TPU v7x, 32 devices: a whole 2x2x4 slice. The times are simulated.
32 devices in a mesh: chan: 8 (over z, y), tm: 4 (over x, core).
Axes of the slice: x: 2, y: 2, z: 4, core: 2. Of those that a mesh axis runs over, the one named last changes fastest.
Arguments:
- traces: float32 [640, 8192], P('chan', 'tm'), may hold values from -6 to 6
- fir_taps: float32 [65], replicated, may hold values from -0.75 to 0.75
- source_index: int32 [64], replicated, may hold values from 0 to 639, as said below
Outputs:
- correlation: float32 [4, 64, 640, 512], P('tm', None, 'chan')
Inputs may be any that keep to these rules, and one draw needn't show every extreme that they name: `source_index`: the 64 channel numbers are distinct. They lie in 8 consecutive blocks of 80 channels (block b holding channels b * 80 to b * 80 + 79, counted around the fibre's end), at most 12 in one block, and exactly 12 in some block. Channels 0 and 639 are always among them.
All inputs are finite; a program needn't handle non-finite values.
Results may differ from a plain program's by a relative error of at most 0.0029.
Values may be sent and summed in bfloat16 or wider, within the bound.
No kernel may reach another device: no remote copies, remote signals or barrier semaphores. Data moves between devices by JAX's collectives and lax.ppermute only.
A program may use at most 192 MiB of HBM per device.

v0:
```python
import math

import jax
import jax.numpy as jnp
from jax import lax
from jax.sharding import PartitionSpec as P

LAG_HALF = 256
NORM_HALF = 64
MAX_OWN = 12


EPSILON = 1e-05


def extended_2(block, sides, width):
    for axis, dim in sides:
        count = lax.axis_size(axis)
        forward = [(i, i + 1) for i in range(count - 1)]
        backward = [(target, source) for source, target in forward]
        low = lax.ppermute(
            lax.slice_in_dim(block, block.shape[dim] - width, None, axis=dim), axis, forward
        )
        high = lax.ppermute(lax.slice_in_dim(block, 0, width, axis=dim), axis, backward)
        block = jnp.concatenate([low, block, high], axis=dim)
    return block


def bandpass(padded, fir_taps):
    result = lax.conv_general_dilated(
        padded[:, None, :],
        fir_taps[None, None, :],
        (1,),
        "VALID",
        dimension_numbers=("NCH", "OIH", "NCH"),
        precision=lax.Precision.HIGHEST,
    )
    return result[:, 0, :]


def body(traces, fir_taps, source_index):
    channels, samples = traces.shape
    fir_half = (fir_taps.shape[0] - 1) // 2
    norm_half = NORM_HALF
    padded = extended_2(traces, (("tm", 1),), fir_half)
    filtered = bandpass(padded, fir_taps)
    filtered_wide = extended_2(filtered, (("tm", 1),), norm_half)
    window_sum = lax.reduce_window(
        jnp.abs(filtered_wide),
        jnp.zeros((), filtered_wide.dtype),
        lax.add,
        (1, 2 * norm_half + 1),
        (1, 1),
        "VALID",
    )
    normed = (filtered / (EPSILON + window_sum / (2 * norm_half + 1))).astype(jnp.bfloat16)
    own_block = lax.axis_index("chan")
    source_total = source_index.shape[0]
    owner = source_index // channels
    offset = source_index - owner * channels
    same_owner = owner[:, None] == owner[None, :]
    earlier = jnp.arange(source_total)[None, :] < jnp.arange(source_total)[:, None]
    rank = jnp.sum((same_owner & earlier).astype(jnp.int32), axis=1)
    slot_number = jnp.arange(MAX_OWN, dtype=jnp.int32)
    match = (owner[None, :] == own_block) & (rank[None, :] == slot_number[:, None])
    slot_offset = jnp.sum(jnp.where(match, offset[None, :], 0), axis=1)
    filled = jnp.any(match, axis=1)
    packed = jnp.where(
        filled[:, None], jnp.take(normed, slot_offset, axis=0), jnp.zeros((), jnp.bfloat16)
    )
    gathered = lax.all_gather(packed, "chan", axis=0, tiled=True)
    sources = jnp.take(gathered, owner * MAX_OWN + rank, axis=0)
    lag_half = LAG_HALF
    extended = extended_2(sources, (("tm", 1),), lag_half)
    lag_width = min(128, 2 * lag_half)
    block_total = 2 * lag_half // lag_width
    shifted = jnp.pad(normed, ((0, 0), (lag_width, lag_width)))
    hankel = jnp.stack(
        [shifted[:, lag_width - j : lag_width - j + samples + lag_width] for j in range(lag_width)],
        axis=1,
    )
    windows = jnp.stack(
        [
            extended[:, i * lag_width : i * lag_width + samples + lag_width]
            for i in range(block_total)
        ],
        axis=0,
    )
    products = jnp.einsum("asu,cju->scaj", windows, hankel, preferred_element_type=jnp.float32)
    correlation = products.reshape(source_total, channels, 2 * lag_half) / math.sqrt(samples)
    return correlation[None]


def solution(mesh):
    placed = (P("chan", "tm"), P(), P())
    return jax.shard_map(
        body, mesh=mesh, in_specs=placed, out_specs=P("tm", None, "chan", None), check_vma=False
    )
```

profile of v0, /device:TPU:1, one launch (start us, length us, event | category | flops | bytes accessed | tf_op | source)
XLA Modules:
  0.0 427.4 jit_solution(8738817306515845697)
XLA Ops:
  0.0 1.4 copy.39
  1.4 4.5 %collective-permute-start = (f32[80,32]{0,1:T(8,128)S(1)}, f32[80,32]{0,1:T(8,128)S(1)}, u32[]{:S(2)}, u32[]{:S(2)}) collective-permute-start(f32[80,32]{0,1:T(8,128)S(1)} %get-tuple-element.9), channel_id=1, source_target_pairs={{0,1},{1,2},{2,3},{4,5},{5,6},{6,7},{8,9},{9,10},{10,11},{12,13},{... | collective-permute-start | bytes 30728 | tf_op jit(solution)/shard_map/ppermute | solution.py:21
  6.0 1.9 collective-permute-start.1
  11.1 158.8 %fusion.24 = f32[80,1,2048]{0,1,2:T(1,128)S(1)} fusion(f32[80,1,2112]{0,1,2:T(1,128)S(1)} %bitcast.290, f32[1,1,65]{1,0,2:T(1,128)S(1)} %copy.42), kind=kOutput, calls=%fused_computation.178 | convolution fusion | flops 127795200 | bytes 1331460 | tf_op jit(solution)/shard_map/conv_general_dilated | solution.py:30
  170.6 3.1 collective-permute-start.2
  173.7 2.1 collective-permute-start.3
  175.8 3.2 collective-permute-done.3
  179.4 37.1 %reduce_window.7 = f32[80,2048]{1,0:T(8,128)S(1)} reduce-window(f32[80,2176]{1,0:T(8,128)S(1)} %abs.3, f32[]{:T(128)} %constant.29.clone.1), window={size=1x129}, to_apply=%region_0.0 | reduce-window | flops 20971520 | bytes 1351684 | tf_op jit(solution)/shard_map/reduce_window | solution.py:48
  221.9 0.9 bitcast_dynamic-update-slice_fusion.121
  229.1 0.9 bitcast_dynamic-update-slice_fusion.113
  233.6 0.9 bitcast_dynamic-update-slice_fusion.108
  238.2 0.9 bitcast_dynamic-update-slice_fusion.103
  240.0 0.9 bitcast_dynamic-update-slice_fusion.101
  245.4 0.9 bitcast_dynamic-update-slice_fusion.95
  250.0 0.9 bitcast_dynamic-update-slice_fusion.90
  254.5 0.9 bitcast_dynamic-update-slice_fusion.85
  256.3 0.9 bitcast_dynamic-update-slice_fusion.83
  265.3 0.9 bitcast_dynamic-update-slice_fusion.73
  267.2 1.1 bitcast_dynamic-update-slice_fusion.71
  281.8 0.9 bitcast_dynamic-update-slice_fusion.55
  283.6 0.9 bitcast_dynamic-update-slice_fusion.53
  287.3 0.9 bitcast_dynamic-update-slice_fusion.49
  294.5 0.9 bitcast_dynamic-update-slice_fusion.41
  320.6 0.9 bitcast_dynamic-update-slice_fusion.12
  329.6 1.1 bitcast_dynamic-update-slice_fusion.2
  332.3 26.4 %all-gather = bf16[8,12,2048]{2,1,0:T(8,128)(2,1)S(1)} all-gather(bf16[1,12,2048]{2,1,0:T(8,128)(2,1)S(1)} %select_bitcast_fusion), channel_id=1, replica_groups=mesh['chan'=8,'tm'=4] {'chan'}, dimensions={0}, use_global_device_ids=true | all-gather | bytes 442368 | tf_op jit(solution)/shard_map/all_gather | solution.py:71
  359.7 7.2 %collective-permute-start.4 = (bf16[64,256]{1,0:T(8,128)(2,1)S(1)}, bf16[64,256]{1,0:T(8,128)(2,1)S(1)}, u32[]{:S(2)}, u32[]{:S(2)}) collective-permute-start(bf16[64,256]{1,0:T(8,128)(2,1)S(1)} %get-tuple-element.19), channel_id=1, source_target_pairs={{0,1},{1,2},{2,3},{4,5},{5,6},{6,7},{8,9},{9,10},{10,11},{12,13},{... | collective-permute-start | bytes 98312 | tf_op jit(solution)/shard_map/ppermute | solution.py:21
  366.9 1.9 collective-permute-start.5
  369.7 2.4 collective-permute-done.5
  372.2 27.3 %multiply_bitcast_fusion = f32[64,80,4,128]{1,0,2,3:T(8,128)} fusion(bf16[80,128,2176]{2,0,1:T(8,128)(2,1)} %bitcast_dynamic-update-slice_fusion, bf16[1,64,2176]{2,1,0:T(8,128)(2,1)S(1)} %get-tuple-element.17, bf16[1,64,2176]{2,1,0:T(8,128)(2,1)S(1)} %get-tuple-element.18, bf16[1,64,2176]{2,1,0:T(8,128)(2,1)S(1)} %get-tuple-element.14, ...), kind=kOutput, calls=%fused_computation.4 | convolution fusion | flops 11415584768 | bytes 56164352 | tf_op jit(solution)/shard_map/asu,cju->scaj/dot_general | solution.py:89
  399.5 14.8 %copy.44 = f32[64,80,4,128]{3,2,1,0:T(4,128)} copy(f32[64,80,4,128]{1,0,2,3:T(8,128)} %multiply_bitcast_fusion) | data formatting | bytes 20971520 | tf_op jit(solution)/shard_map/div | solution.py:90
  414.3 12.7 %div.32 = f32[1,64,80,512]{3,2,1,0:T(8,128)} reshape(f32[64,80,4,128]{3,2,1,0:T(4,128)} %copy.44) | data formatting | bytes 20971520 | tf_op jit(solution)/shard_map/div | solution.py:90
  (140 shorter events, 105.8 us)
Async XLA Ops:
  1.4 9.0 %collective-permute-start = (f32[80,32]{0,1:T(8,128)S(1)}, f32[80,32]{0,1:T(8,128)S(1)}, u32[]{:S(2)}, u32[]{:S(2)}) collective-permute-start(f32[80,32]{0,1:T(8,128)S(1)} %get-tuple-element.9), channel_id=1, source_target_pairs={{0,1},{1,2},{2,3},{4,5},{5,6},{6,7},{8,9},{9,10},{10,11},{12,13},{... | collective-permute-start | bytes 30728 | tf_op jit(solution)/shard_map/ppermute | solution.py:21
  6.0 5.1 %collective-permute-start.1 = (f32[80,32]{0,1:T(8,128)S(1)}, f32[80,32]{0,1:T(8,128)S(1)}, u32[]{:S(2)}, u32[]{:S(2)}) collective-permute-start(f32[80,32]{0,1:T(8,128)S(1)} %get-tuple-element.10), channel_id=1, source_target_pairs={{1,0},{2,1},{3,2},{5,4},{6,5},{7,6},{9,8},{10,9},{11,10},{13,12},{... | collective-permute-start | bytes 30728 | tf_op jit(solution)/shard_map/ppermute | solution.py:24
  170.6 5.2 %collective-permute-start.2 = (f32[80,64]{1,0:T(8,128)S(1)}, f32[80,64]{1,0:T(8,128)S(1)}, u32[]{:S(2)}, u32[]{:S(2)}) collective-permute-start(f32[80,64]{1,0:T(8,128)S(1)} %get-tuple-element.12), channel_id=1, source_target_pairs={{0,1},{1,2},{2,3},{4,5},{5,6},{6,7},{8,9},{9,10},{10,11},{12,13},{... | collective-permute-start | bytes 61448 | tf_op jit(solution)/shard_map/ppermute | solution.py:21
  173.7 5.3 %collective-permute-start.3 = (f32[80,64]{1,0:T(8,128)S(1)}, f32[80,64]{1,0:T(8,128)S(1)}, u32[]{:S(2)}, u32[]{:S(2)}) collective-permute-start(f32[80,64]{1,0:T(8,128)S(1)} %get-tuple-element.11), channel_id=1, source_target_pairs={{1,0},{2,1},{3,2},{5,4},{6,5},{7,6},{9,8},{10,9},{11,10},{13,12},{... | collective-permute-start | bytes 61448 | tf_op jit(solution)/shard_map/ppermute | solution.py:24
  359.7 10.0 %collective-permute-start.4 = (bf16[64,256]{1,0:T(8,128)(2,1)S(1)}, bf16[64,256]{1,0:T(8,128)(2,1)S(1)}, u32[]{:S(2)}, u32[]{:S(2)}) collective-permute-start(bf16[64,256]{1,0:T(8,128)(2,1)S(1)} %get-tuple-element.19), channel_id=1, source_target_pairs={{0,1},{1,2},{2,3},{4,5},{5,6},{6,7},{8,9},{9,10},{10,11},{12,13},{... | collective-permute-start | bytes 98312 | tf_op jit(solution)/shard_map/ppermute | solution.py:21
  366.9 5.2 %collective-permute-start.5 = (bf16[64,256]{1,0:T(8,128)(2,1)S(1)}, bf16[64,256]{1,0:T(8,128)(2,1)S(1)}, u32[]{:S(2)}, u32[]{:S(2)}) collective-permute-start(bf16[64,256]{1,0:T(8,128)(2,1)S(1)} %get-tuple-element.20), channel_id=1, source_target_pairs={{1,0},{2,1},{3,2},{5,4},{6,5},{7,6},{9,8},{10,9},{11,10},{13,12},{... | collective-permute-start | bytes 98312 | tf_op jit(solution)/shard_map/ppermute | solution.py:24
where the time goes:
time: 435 us; the launch traced here: 427 us
  matrix products  186 us (43%)
  local copies, waits for them, and re-layouts  148 us (34%)
  other arithmetic  39.4 us (9%)
  blocking collectives  26.4 us (6%)
  starting transfers between devices  20.7 us (5%)
  waiting for transfers between devices  6.17 us (1%)
    conv_general_dilated x1, matrix products, bandpass(): lax.conv_general_dilated(padded[:, None, :], fir_taps[None, None, :], (1,...  159 us
    unnamed x129, local copies, waits for them, and re-layouts  116 us
    another operation x1, other arithmetic, body(): lax.reduce_window(jnp.abs(filtered_wide), jnp.zeros((), filtered_wide.dty...  37.1 us
    div x2, local copies, waits for them, and re-layouts, body(): products.reshape(source_total, channels, 2 * lag_half) / math.sqrt(samples)  27.5 us
    dot_general x1, matrix products, body(): jnp.einsum('asu,cju->scaj', windows, hankel, preferred_element_type=jnp.f...  27.3 us
    all_gather x1, blocking collectives, body(): gathered = lax.all_gather(packed, 'chan', axis=0, tiled=True)  26.4 us
    ppermute x3, starting transfers between devices, extended_2(): lax.ppermute(lax.slice_in_dim(block, block.shape[dim] - width, None, axis...  14.8 us
  transfers between devices with their start and end apart: 6, of which 3 were waited for; matrix products, arithmetic and copies ran while one was open for 1% of the time, Pallas kernels for 0%

commit v1 on v0

v1 whole, which is shorter than its diff:
```python
import functools
import math

import jax
import jax.numpy as jnp
from jax import lax
from jax.experimental import pallas as pl
from jax.experimental.pallas import tpu as pltpu
from jax.sharding import PartitionSpec as P

LAG_HALF = 256
NORM_HALF = 64
MAX_OWN = 12
EPSILON = 1e-05

LANES = 128
LAG_WIDTH = 32
PIECES = LANES // LAG_WIDTH
LAG_BLOCKS = 2 * LAG_HALF // LANES
SIDE = 3
EDGE = LAG_HALF // LANES
GROUP = 8
MIB = 2**20
F32 = jnp.float32
BF16 = jnp.bfloat16


def split(value):
    high = value.astype(BF16)
    return high, (value - high.astype(F32)).astype(BF16)


def dot_t(left, right):
    return lax.dot_general(left, right, (((1,), (1,)), ((), ())), preferred_element_type=F32)


def stacked(blocks):
    wide = [
        jnp.concatenate([blocks[b - 1], blocks[b], blocks[b + 1]], axis=1)
        for b in range(1, len(blocks) - 1)
    ]
    return jnp.concatenate(wide, axis=0)


def normalize(blocks, first, last, has_low, has_high, taps_row, fir_taps):
    rows = blocks[0].shape[0]
    row = lax.broadcasted_iota(jnp.int32, (LANES, 3 * LANES), 0)
    lane = lax.broadcasted_iota(jnp.int32, (LANES, 3 * LANES), 1)
    toeplitz = pltpu.roll(jnp.broadcast_to(taps_row, (LANES, 3 * LANES)), 0, 1, stride=1, stride_axis=0)
    taps_high, taps_low = split(toeplitz)
    reach = lane - row - (LANES - NORM_HALF)
    band = jnp.where((reach >= 0) & (reach <= 2 * NORM_HALF), 1.0, 0.0).astype(BF16)
    wide_high, wide_low = [], []
    pairs = [split(block) for block in blocks]
    wide_high = stacked([p[0] for p in pairs])
    wide_low = stacked([p[1] for p in pairs])
    filtered = dot_t(wide_high, taps_high) + dot_t(wide_low, taps_high) + dot_t(wide_high, taps_low)
    inner = []
    for k in range(len(blocks) - 2):
        block = filtered[k * rows : (k + 1) * rows]
        number = first + 1 + k
        if number < 0:
            block = jnp.where(has_low, block, 0.0)
        elif number > last:
            block = jnp.where(has_high, block, 0.0)
        inner.append(block)
    sizes = [split(jnp.abs(block)) for block in inner]
    total = dot_t(stacked([p[0] for p in sizes]), band) + dot_t(stacked([p[1] for p in sizes]), band)
    level = total / (2 * NORM_HALF + 1)
    return [
        block / (EPSILON + level[k * rows : (k + 1) * rows]) for k, block in enumerate(inner[1:-1])
    ]


def source_kernel(offset, place, traces, low, high, taps_row, out, rows_buf, *, fir_taps):
    samples = traces.shape[1]
    own = samples // LANES
    side = low.shape[1]
    rows_buf[...] = jnp.zeros_like(rows_buf)
    for k in range(MAX_OWN):
        at = offset[k]
        rows_buf[k : k + 1, LANES : LANES + side] = low[pl.ds(at, 1), :]
        rows_buf[k : k + 1, LANES + side : LANES + side + samples] = traces[pl.ds(at, 1), :]
        rows_buf[k : k + 1, LANES + side + samples : LANES + 2 * side + samples] = high[pl.ds(at, 1), :]
    count = rows_buf.shape[1] // LANES
    blocks = [rows_buf[:, b * LANES : (b + 1) * LANES] for b in range(count)]
    normed = normalize(
        blocks, -SIDE - 1, own - 1, place[0] > 0, place[0] < place[1] - 1, taps_row[...], fir_taps
    )
    packed = jnp.concatenate([block[:MAX_OWN] for block in normed], axis=0)
    out[...] = packed.astype(BF16)


def shifted_kernel(place, traces, low, high, taps_row, out, rows_buf, *, fir_taps):
    channels, samples = traces.shape
    own = samples // LANES
    side = low.shape[1]
    blocks = [low[:, side - 2 * LANES : side - LANES], low[:, side - LANES :]]
    blocks += [traces[:, b * LANES : (b + 1) * LANES] for b in range(own)]
    blocks += [high[:, :LANES], high[:, LANES : 2 * LANES]]
    normed = normalize(
        blocks, -2, own - 1, place[0] > 0, place[0] < place[1] - 1, taps_row[...], fir_taps
    )
    for b, block in enumerate(normed):
        rows_buf[b * channels : (b + 1) * channels, :] = block
    lane = lax.broadcasted_iota(jnp.int32, (LAG_WIDTH, LANES), 1)
    later = lane >= lax.broadcasted_iota(jnp.int32, (LAG_WIDTH, LANES), 0)

    @pl.loop(0, channels)
    def _(c):
        before = jnp.zeros((LAG_WIDTH, LANES), F32)
        at = pl.multiple_of(c * LAG_WIDTH, LAG_WIDTH)
        for b in range(own + 1):
            if b < own:
                line = rows_buf[pl.ds(b * channels + c, 1), :]
                turned = pltpu.roll(
                    jnp.broadcast_to(line, (LAG_WIDTH, LANES)), 0, 1, stride=1, stride_axis=0
                )
            else:
                turned = jnp.zeros((LAG_WIDTH, LANES), F32)
            out[pl.ds(at, LAG_WIDTH), b * LANES : (b + 1) * LANES] = jnp.where(
                later, turned, before
            ).astype(BF16)
            before = turned


def correlate_kernel(place, *refs, sources, channels, samples, pieces, scale):
    parts = refs[:pieces]
    shifted, out, all_rows, lines, windows, ready, sem = refs[pieces:]
    step = pl.program_id(0)
    slot = lax.rem(step, 2)
    depth = samples + LANES
    blocks = samples // LANES + 2 * EDGE

    def sends(at, slot):
        return [
            pltpu.make_async_copy(
                ready.at[slot, q].reshape(sources, GROUP, LANES),
                out.at[:, pl.ds(at * GROUP, GROUP), pl.ds(q * LANES, LANES)],
                sem.at[slot],
            )
            for q in range(LAG_BLOCKS)
        ]

    @pl.when(step == 0)
    def _():
        start = 0
        for part in parts:
            all_rows[start : start + part.shape[0], :] = part[...].astype(F32)
            start += part.shape[0]
        lines[blocks * sources :, :] = jnp.zeros((sources, LANES), F32)

        for s in range(sources):
            lines[pl.ds(s, blocks, stride=sources), :] = all_rows[
                pl.ds(place[s], blocks, stride=MAX_OWN), :
            ]

        lane = lax.broadcasted_iota(jnp.int32, (sources, LANES), 1)
        for p in range(PIECES):
            turn = p * LAG_WIDTH
            turned = None
            for b in range(blocks + 1):
                line = lines[b * sources : (b + 1) * sources, :]
                following = pltpu.roll(line, LANES - turn, 1) if p else line
                if b:
                    block = b - 1
                    value = jnp.where(lane < LANES - turn, turned, following).astype(BF16)
                    for q in range(LAG_BLOCKS):
                        if 0 <= block - q < depth // LANES:
                            at = (q * PIECES + p) * sources
                            windows[at : at + sources, (block - q) * LANES : (block - q + 1) * LANES] = value
                turned = following

    @pl.when(step >= 2)
    def _():
        for copy in sends(step - 2, slot):
            copy.wait()

    width = GROUP * LAG_WIDTH
    result = dot_t(windows[...], shifted[pl.ds(pl.multiple_of(step * width, width), width), :])
    lane = lax.broadcasted_iota(jnp.int32, (sources, LANES), 1)
    for q in range(LAG_BLOCKS):
        for half in range(width // LANES):
            tiles = [
                result[
                    (q * PIECES + p) * sources : (q * PIECES + p + 1) * sources,
                    half * LANES : (half + 1) * LANES,
                ]
                * scale
                for p in range(PIECES)
            ]
            gap = PIECES // 2
            while gap:
                wide = gap * LAG_WIDTH
                low_half = lax.rem(lane, 2 * wide) < wide
                for p in range(PIECES):
                    if p & gap:
                        continue
                    a, b = tiles[p], tiles[p + gap]
                    tiles[p] = jnp.where(low_half, a, pltpu.roll(b, wide, 1))
                    tiles[p + gap] = jnp.where(low_half, pltpu.roll(a, LANES - wide, 1), b)
                gap //= 2
            for p in range(PIECES):
                ready.at[slot, q][pl.ds(half * PIECES + p, sources, stride=GROUP), :] = tiles[p]
    for copy in sends(step, slot):
        copy.start()

    @pl.when(step == pl.num_programs(0) - 1)
    def _():
        for copy in sends(step - 1, 1 - slot):
            copy.wait()
        for copy in sends(step, slot):
            copy.wait()


SMEM = pl.BlockSpec(memory_space=pltpu.SMEM)
VMEM = pl.BlockSpec(memory_space=pltpu.VMEM)


def source_rows(offset, place, traces, low, high, taps_row, fir_taps):
    samples = traces.shape[1]
    blocks = samples // LANES + 2 * EDGE
    return pl.pallas_call(
        functools.partial(source_kernel, fir_taps=fir_taps),
        in_specs=[SMEM, SMEM] + [VMEM] * 4,
        out_specs=VMEM,
        out_shape=jax.ShapeDtypeStruct((blocks * MAX_OWN, LANES), BF16),
        scratch_shapes=[pltpu.VMEM((16, samples + 2 * (SIDE + 1) * LANES), F32)],
        compiler_params=pltpu.CompilerParams(vmem_limit_bytes=16 * MIB),
        name="source_rows",
    )(offset, place, traces, low, high, taps_row)


def shifted_rows(place, traces, low, high, taps_row, fir_taps):
    channels, samples = traces.shape
    return pl.pallas_call(
        functools.partial(shifted_kernel, fir_taps=fir_taps),
        in_specs=[SMEM] + [VMEM] * 4,
        out_specs=VMEM,
        out_shape=jax.ShapeDtypeStruct((channels * LAG_WIDTH, samples + LANES), BF16),
        scratch_shapes=[pltpu.VMEM((channels * samples // LANES, LANES), F32)],
        compiler_params=pltpu.CompilerParams(vmem_limit_bytes=32 * MIB),
        cost_estimate=pl.CostEstimate(
            flops=2 * 3 * channels * samples * 3 * LANES, bytes_accessed=10 * channels * samples * 2, transcendentals=0
        ),
        name="shifted_rows",
    )(place, traces, low, high, taps_row)


def correlate(place, parts, shifted, sources, channels, samples):
    blocks = samples // LANES + 2 * EDGE
    rows = sum(part.shape[0] for part in parts)
    scale = 1.0 / math.sqrt(samples)
    return pl.pallas_call(
        functools.partial(
            correlate_kernel,
            sources=sources,
            channels=channels,
            samples=samples,
            pieces=len(parts),
            scale=scale,
        ),
        grid=(channels // GROUP,),
        in_specs=[SMEM] + [VMEM] * len(parts) + [VMEM],
        out_specs=pl.BlockSpec(memory_space=pl.ANY),
        out_shape=jax.ShapeDtypeStruct((sources, channels, 2 * LAG_HALF), F32),
        scratch_shapes=[
            pltpu.VMEM((rows, LANES), F32),
            pltpu.VMEM(((blocks + 1) * sources, LANES), F32),
            pltpu.VMEM((LAG_BLOCKS * PIECES * sources, samples + LANES), BF16),
            pltpu.VMEM((2, LAG_BLOCKS, sources * GROUP, LANES), F32),
            pltpu.SemaphoreType.DMA((2,)),
        ],
        compiler_params=pltpu.CompilerParams(vmem_limit_bytes=48 * MIB),
        name="correlate",
    )(place, *parts, shifted)


def body(traces, fir_taps, source_index):
    channels, samples = traces.shape
    taps = fir_taps.shape[0]
    width = SIDE * LANES
    slabs = lax.axis_size("tm")
    blocks_of = lax.axis_size("chan")
    forward = [(i, i + 1) for i in range(slabs - 1)]
    low = lax.ppermute(traces[:, samples - width :], "tm", forward)
    high = lax.ppermute(traces[:, :width], "tm", [(b, a) for a, b in forward])

    me = lax.axis_index("chan")
    sources = source_index.shape[0]
    owner = source_index // channels
    offset = source_index - owner * channels
    number = jnp.arange(sources)
    same = (owner[:, None] == owner[None, :]) & (number[None, :] < number[:, None])
    rank = jnp.sum(same.astype(jnp.int32), axis=1)
    match = (owner[None, :] == me) & (rank[None, :] == jnp.arange(MAX_OWN, dtype=jnp.int32)[:, None])
    slot_offset = jnp.sum(jnp.where(match, offset[None, :], 0), axis=1)
    place = jnp.stack([lax.axis_index("tm"), jnp.int32(slabs)]).astype(jnp.int32)
    lead = LANES - (taps - 1) // 2
    taps_row = jnp.pad(fir_taps, (lead, 3 * LANES - lead - taps))[None]

    own = source_rows(slot_offset, place, traces, low, high, taps_row, taps)
    shifted = shifted_rows(place, traces, low, high, taps_row, taps)
    if blocks_of == 8:
        def swap(value, distance):
            return lax.ppermute(value, "chan", [(i, i ^ distance) for i in range(blocks_of)])

        z3, z2, z1 = swap(own, 6), swap(own, 4), swap(own, 2)
        y = swap(own, 1)
        column = jnp.concatenate([z1, z2, z3], axis=0)
        other = swap(column, 1)
        parts = [own, y, column, other]
        apart = owner ^ me
        half = apart // 2
        piece = jnp.where(half == 0, apart, 1 + half + 3 * (apart % 2))
    else:
        parts = [lax.all_gather(own, "chan", axis=0, tiled=True)]
        piece = owner
    start = (piece * own.shape[0] + rank).astype(jnp.int32)
    return correlate(start, parts, shifted, sources, channels, samples)[None]


def solution(mesh):
    placed = (P("chan", "tm"), P(), P())
    return jax.shard_map(
        body, mesh=mesh, in_specs=placed, out_specs=P("tm", None, "chan", None), check_vma=False
    )
```

time: 435 us -> 65.3 us (0.15)
  the two profiles are of different devices: /device:TPU:1 before, /device:TPU:0 now
where the time goes in v1:
time: 65.3 us; the launch traced here: 65 us
  Pallas kernels  36.2 us (55%)
  starting transfers between devices  12.1 us (19%)
  local copies, waits for them, and re-layouts  8.11 us (12%)
  waiting for transfers between devices  6.81 us (10%)
  other arithmetic  1.72 us (3%)
    pallas_call x1, Pallas kernels, correlate(): pl.pallas_call(functools.partial(correlate_kernel, sources=sources, chann...  24.1 us
    pallas_call x1, Pallas kernels, shifted_rows(): pl.pallas_call(functools.partial(shifted_kernel, fir_taps=fir_taps), in_s...  10.8 us
    ppermute x5, starting transfers between devices, swap(): lax.ppermute(value, 'chan', [(i, i ^ distance) for i in range(blocks_of)])  7.77 us
    ppermute x5, waiting for transfers between devices, swap(): lax.ppermute(value, 'chan', [(i, i ^ distance) for i in range(blocks_of)])  6.8 us
    unnamed x8, local copies, waits for them, and re-layouts  6.38 us
    ppermute x1, starting transfers between devices, body(): low = lax.ppermute(traces[:, samples - width:], 'tm', forward)  3.04 us
  transfers between devices with their start and end apart: 7, of which 1 were waited for; matrix products, arithmetic and copies ran while one was open for 4% of the time, Pallas kernels for 17%

profile of v1, /device:TPU:0, one launch (start us, length us, event | category | flops | bytes accessed | tf_op | source)
XLA Modules:
  0.0 65.0 jit_solution(11626483424615780573)
XLA Ops:
  0.0 1.0 %fusion.6 = (f32[80,384]{1,0:T(8,128)S(1)}, f32[80,384]{1,0:T(8,128)S(1)}) fusion(f32[80,2048]{1,0:T(8,128)} %traces.3), kind=kLoop, calls=%fused_computation.23 | loop fusion | bytes 491520 | tf_op jit(solution)/shard_map/slice | solution.py:287
  1.0 1.3 %collective-permute-start.1 = (f32[80,384]{1,0:T(8,128)S(1)}, f32[80,384]{1,0:T(8,128)S(1)}, u32[]{:S(2)}, u32[]{:S(2)}) collective-permute-start(f32[80,384]{1,0:T(8,128)S(1)} %get-tuple-element.7), channel_id=1, source_target_pairs={{1,0},{2,1},{3,2},{5,4},{6,5},{7,6},{9,8},{10,9},{11,10},{13,12},{... | collective-permute-start | bytes 368648 | tf_op jit(solution)/shard_map/ppermute | solution.py:287
  2.3 3.0 %collective-permute-start = (f32[80,384]{1,0:T(8,128)S(1)}, f32[80,384]{1,0:T(8,128)S(1)}, u32[]{:S(2)}, u32[]{:S(2)}) collective-permute-start(f32[80,384]{1,0:T(8,128)S(1)} %get-tuple-element.8), channel_id=1, source_target_pairs={{0,1},{1,2},{2,3},{4,5},{5,6},{6,7},{8,9},{9,10},{10,11},{12,13},{... | collective-permute-start | bytes 368648 | tf_op jit(solution)/shard_map/ppermute | solution.py:286
  5.3 0.7 %broadcast_compare_fusion = (pred[64]{0:T(512)(128)(4,1)S(1)}, s32[64]{0:T(128)S(1)}) fusion(s32[]{:T(128)S(6)} %axis_index.23, s32[64]{0:T(128)} %param.5), kind=kLoop, calls=%fused_computation.22 | loop fusion | flops 576 | bytes 580 | tf_op jit(solution)/shard_map/eq | solution.py:296
  6.0 0.2 convert_reduce_fusion
  6.2 0.7 %multiply_subtract_fusion = (s32[64]{0:T(128)S(1)}, s32[64]{0:T(128)S(1)}) fusion(s32[64]{0:T(128)} %param.5, s32[64]{0:T(128)S(1)} %get-tuple-element.6, s32[64]{0:T(128)S(1)} %convert_reduce_fusion, s32[]{:T(128)S(6)} %axis_index.23), kind=kLoop, calls=%fused_computation.21 | loop fusion | flops 1856 | bytes 1284 | tf_op jit(solution)/shard_map/sub | solution.py:292
  6.9 0.1 pad_add_fusion.place
  6.9 0.7 %pad.4 = f32[384]{0:T(512)S(1)} pad(f32[65]{0:T(128)} %param.4, f32[]{:T(128)} %constant.52.clone.1), padding=96_223 | pad | bytes 1800 | tf_op jit(solution)/shard_map/jit(_pad)/pad | solution.py:300
  7.7 0.1 select_reduce_fusion.offset
  7.8 0.0 collective-permute-done.1.high
  7.8 0.0 collective-permute-done.low
  7.8 0.0 copy-start.1
  7.8 1.1 %copy-done.1 = f32[80,2048]{1,0:T(8,128)S(1)} copy-done((f32[80,2048]{1,0:T(8,128)S(1)}, f32[80,2048]{1,0:T(8,128)}, u32[]{:S(2)}) %copy-start.1) | copy-done | bytes 655384
  8.9 1.3 %source_rows.1.refs_0_ = bf16[240,128]{1,0:T(8,128)(2,1)S(1)} custom-call(s32[12]{0:T(128)S(1)} %select_reduce_fusion.offset, s32[2]{0:T(128)S(1)} %pad_add_fusion.place, f32[80,2048]{1,0:T(8,128)S(1)} %copy-done.1, f32[80,384]{1,0:T(8,128)S(1)} %collective-permute-done.low, f32[80,384]{1,0:T(8,128)S(1)} %collective-permute-done.1.high, ...), custom_call_target="tpu_custom_call" | custom-call | tf_op jit(solution)/shard_map/source_rows/pallas_call | solution.py:223
  10.2 3.1 %collective-permute-start.3 = (bf16[240,128]{1,0:T(8,128)(2,1)S(1)}, bf16[240,128]{1,0:T(8,128)(2,1)S(1)}, u32[]{:S(2)}, u32[]{:S(2)}) collective-permute-start(bf16[240,128]{1,0:T(8,128)(2,1)S(1)} %source_rows.1.refs_0_), channel_id=1, source_target_pairs={{0,8},{4,12},{8,0},{12,4},{16,24},{20,28},{24,16},{28,20},{1,9},{5... | collective-permute-start | bytes 184328 | tf_op jit(solution)/shard_map/ppermute | solution.py:306
  13.3 2.5 %collective-permute-start.5 = (bf16[240,128]{1,0:T(8,128)(2,1)S(1)}, bf16[240,128]{1,0:T(8,128)(2,1)S(1)}, u32[]{:S(2)}, u32[]{:S(2)}) collective-permute-start(bf16[240,128]{1,0:T(8,128)(2,1)S(1)} %source_rows.1.refs_0_), channel_id=1, source_target_pairs={{0,24},{4,28},{8,16},{12,20},{16,8},{20,12},{24,0},{28,4},{1,25},{... | collective-permute-start | bytes 184328 | tf_op jit(solution)/shard_map/ppermute | solution.py:306
  15.8 0.1 collective-permute-start.4
  15.9 0.0 collective-permute-done.3
  15.9 6.8 %collective-permute-done.4 = bf16[240,128]{1,0:T(8,128)(2,1)S(1)} collective-permute-done((bf16[240,128]{1,0:T(8,128)(2,1)S(1)}, bf16[240,128]{1,0:T(8,128)(2,1)S(1)}, u32[]{:S(2)}, u32[]{:S(2)}) %collective-permute-start.4) | collective-permute-done | bytes 61472 | tf_op jit(solution)/shard_map/ppermute | solution.py:306
  22.7 0.0 collective-permute-done.5
  22.7 1.6 %collective-permute-start.6 = (bf16[720,128]{1,0:T(8,128)(2,1)S(1)}, bf16[720,128]{1,0:T(8,128)(2,1)S(1)}, u32[]{:S(2)}, u32[]{:S(2)}) collective-permute-start(bf16[720,128]{1,0:T(8,128)(2,1)S(1)} %constant_dynamic-update-slice_fusion.refs_2_), channel_id=1, source_target_pairs={{0,4},{4,0},{8,12},{12,8},{16,20},{20,16},{24,28},{28,24},{1,5},{5... | collective-permute-start | bytes 552968 | tf_op jit(solution)/shard_map/ppermute | solution.py:306
  24.3 0.5 collective-permute-start.2
  24.8 0.0 copy-start.2
  24.8 1.1 %copy-done.2 = f32[80,2048]{1,0:T(8,128)S(1)} copy-done((f32[80,2048]{1,0:T(8,128)S(1)}, f32[80,2048]{1,0:T(8,128)}, u32[]{:S(2)}) %copy-start.2) | copy-done | bytes 655384
  25.9 10.8 %shifted_rows.1.refs_4_ = bf16[2560,2176]{1,0:T(8,128)(2,1)S(1)} custom-call(s32[2]{0:T(128)S(1)} %pad_add_fusion.place, f32[80,2048]{1,0:T(8,128)S(1)} %copy-done.2, f32[80,384]{1,0:T(8,128)S(1)} %collective-permute-done.low, f32[80,384]{1,0:T(8,128)S(1)} %collective-permute-done.1.high, f32[1,384]{1,0:T(1,128)S(1)} %broadcast_in_dim.28.taps_row), custom_call_target="tpu_custom_call" | custom-call | flops 377487360 | bytes 3276800 | tf_op jit(solution)/shard_map/shifted_rows/pallas_call | solution.py:236
  36.7 0.0 copy-start
  36.7 4.2 %copy-done = bf16[2560,2176]{1,0:T(8,128)(2,1)} copy-done((bf16[2560,2176]{1,0:T(8,128)(2,1)}, bf16[2560,2176]{1,0:T(8,128)(2,1)S(1)}, u32[]{:S(2)}) %copy-start) | copy-done | bytes 11141144
  40.9 0.0 collective-permute-done.2.refs_1_
  40.9 0.0 collective-permute-done.6.refs_3_
  40.9 24.1 %correlate.1 = f32[64,80,512]{2,1,0:T(8,128)} custom-call(s32[64]{0:T(128)S(1)} %get-tuple-element.10.place, bf16[240,128]{1,0:T(8,128)(2,1)S(1)} %source_rows.1.refs_0_, bf16[240,128]{1,0:T(8,128)(2,1)S(1)} %collective-permute-done.2.refs_1_, bf16[720,128]{1,0:T(8,128)(2,1)S(1)} %constant_dynamic-update-slice_fusion.refs_2_, ...), custom_call_target="tpu_custom_call" | custom-call | tf_op jit(solution)/shard_map/correlate/pallas_call | solution.py:254
  (4 shorter events, 0.0 us)
Async XLA Ops:
  1.0 6.8 %collective-permute-start.1 = (f32[80,384]{1,0:T(8,128)S(1)}, f32[80,384]{1,0:T(8,128)S(1)}, u32[]{:S(2)}, u32[]{:S(2)}) collective-permute-start(f32[80,384]{1,0:T(8,128)S(1)} %get-tuple-element.7), channel_id=1, source_target_pairs={{1,0},{2,1},{3,2},{5,4},{6,5},{7,6},{9,8},{10,9},{11,10},{13,12},{... | collective-permute-start | bytes 368648 | tf_op jit(solution)/shard_map/ppermute | solution.py:287
  2.3 5.5 %collective-permute-start = (f32[80,384]{1,0:T(8,128)S(1)}, f32[80,384]{1,0:T(8,128)S(1)}, u32[]{:S(2)}, u32[]{:S(2)}) collective-permute-start(f32[80,384]{1,0:T(8,128)S(1)} %get-tuple-element.8), channel_id=1, source_target_pairs={{0,1},{1,2},{2,3},{4,5},{5,6},{6,7},{8,9},{9,10},{10,11},{12,13},{... | collective-permute-start | bytes 368648 | tf_op jit(solution)/shard_map/ppermute | solution.py:286
  7.8 1.1 %copy-start.1 = (f32[80,2048]{1,0:T(8,128)S(1)}, f32[80,2048]{1,0:T(8,128)}, u32[]{:S(2)}) copy-start(f32[80,2048]{1,0:T(8,128)} %traces.3) | copy-start | bytes 1966084
  10.2 5.7 %collective-permute-start.3 = (bf16[240,128]{1,0:T(8,128)(2,1)S(1)}, bf16[240,128]{1,0:T(8,128)(2,1)S(1)}, u32[]{:S(2)}, u32[]{:S(2)}) collective-permute-start(bf16[240,128]{1,0:T(8,128)(2,1)S(1)} %source_rows.1.refs_0_), channel_id=1, source_target_pairs={{0,8},{4,12},{8,0},{12,4},{16,24},{20,28},{24,16},{28,20},{1,9},{5... | collective-permute-start | bytes 184328 | tf_op jit(solution)/shard_map/ppermute | solution.py:306
  13.3 9.4 %collective-permute-start.5 = (bf16[240,128]{1,0:T(8,128)(2,1)S(1)}, bf16[240,128]{1,0:T(8,128)(2,1)S(1)}, u32[]{:S(2)}, u32[]{:S(2)}) collective-permute-start(bf16[240,128]{1,0:T(8,128)(2,1)S(1)} %source_rows.1.refs_0_), channel_id=1, source_target_pairs={{0,24},{4,28},{8,16},{12,20},{16,8},{20,12},{24,0},{28,4},{1,25},{... | collective-permute-start | bytes 184328 | tf_op jit(solution)/shard_map/ppermute | solution.py:306
  15.8 6.9 %collective-permute-start.4 = (bf16[240,128]{1,0:T(8,128)(2,1)S(1)}, bf16[240,128]{1,0:T(8,128)(2,1)S(1)}, u32[]{:S(2)}, u32[]{:S(2)}) collective-permute-start(bf16[240,128]{1,0:T(8,128)(2,1)S(1)} %source_rows.1.refs_0_), channel_id=1, source_target_pairs={{0,16},{4,20},{8,24},{12,28},{16,0},{20,4},{24,8},{28,12},{1,17},{... | collective-permute-start | bytes 184328 | tf_op jit(solution)/shard_map/ppermute | solution.py:306
  22.7 18.2 %collective-permute-start.6 = (bf16[720,128]{1,0:T(8,128)(2,1)S(1)}, bf16[720,128]{1,0:T(8,128)(2,1)S(1)}, u32[]{:S(2)}, u32[]{:S(2)}) collective-permute-start(bf16[720,128]{1,0:T(8,128)(2,1)S(1)} %constant_dynamic-update-slice_fusion.refs_2_), channel_id=1, source_target_pairs={{0,4},{4,0},{8,12},{12,8},{16,20},{20,16},{24,28},{28,24},{1,5},{5... | collective-permute-start | bytes 552968 | tf_op jit(solution)/shard_map/ppermute | solution.py:306
  24.3 16.6 %collective-permute-start.2 = (bf16[240,128]{1,0:T(8,128)(2,1)S(1)}, bf16[240,128]{1,0:T(8,128)(2,1)S(1)}, u32[]{:S(2)}, u32[]{:S(2)}) collective-permute-start(bf16[240,128]{1,0:T(8,128)(2,1)S(1)} %source_rows.1.refs_0_), channel_id=1, source_target_pairs={{0,4},{4,0},{8,12},{12,8},{16,20},{20,16},{24,28},{28,24},{1,5},{5... | collective-permute-start | bytes 184328 | tf_op jit(solution)/shard_map/ppermute | solution.py:306
  24.8 1.1 %copy-start.2 = (f32[80,2048]{1,0:T(8,128)S(1)}, f32[80,2048]{1,0:T(8,128)}, u32[]{:S(2)}) copy-start(f32[80,2048]{1,0:T(8,128)} %traces.3) | copy-start | bytes 1966084
  36.7 4.2 %copy-start = (bf16[2560,2176]{1,0:T(8,128)(2,1)}, bf16[2560,2176]{1,0:T(8,128)(2,1)S(1)}, u32[]{:S(2)}) copy-start(bf16[2560,2176]{1,0:T(8,128)(2,1)S(1)} %shifted_rows.1.refs_4_) | copy-start | bytes 33423364

commit v2 on v1

--- a/solution.py
+++ b/solution.py
@@ -20,6 +20,8 @@
 SIDE = 3
 EDGE = LAG_HALF // LANES
 GROUP = 8
+TILE = 256
+UNITS = 2
 MIB = 2**20
 F32 = jnp.float32
 BF16 = jnp.bfloat16
@@ -106,7 +108,11 @@
     lane = lax.broadcasted_iota(jnp.int32, (LAG_WIDTH, LANES), 1)
     later = lane >= lax.broadcasted_iota(jnp.int32, (LAG_WIDTH, LANES), 0)
 
-    @pl.loop(0, channels)
+    beyond = samples + LANES
+    if out.shape[1] > beyond:
+        out[:, beyond:] = jnp.zeros((out.shape[0], out.shape[1] - beyond), BF16)
+
+    @pl.loop(0, channels, unroll=8)
     def _(c):
         before = jnp.zeros((LAG_WIDTH, LANES), F32)
         at = pl.multiple_of(c * LAG_WIDTH, LAG_WIDTH)
@@ -124,71 +130,45 @@
             before = turned
 
 
-def correlate_kernel(place, *refs, sources, channels, samples, pieces, scale):
+def correlate_kernel(*refs, sources, **sizes):
+    tiles_of = LAG_BLOCKS * PIECES
+
+    def run(*sums):
+        split_sums = [sums[m * tiles_of : (m + 1) * tiles_of] for m in range(UNITS)]
+        correlate_steps(split_sums, *refs, sources=sources, **sizes)
+
+    pl.run_scoped(
+        run, *[pltpu.ACC(m)((sources, TILE), F32) for m in range(UNITS) for _ in range(tiles_of)]
+    )
+
+
+def correlate_steps(sums, place, *refs, sources, channels, samples, pieces, scale):
     parts = refs[:pieces]
     shifted, out, all_rows, lines, windows, ready, sem = refs[pieces:]
     step = pl.program_id(0)
-    slot = lax.rem(step, 2)
-    depth = samples + LANES
+    steps = pl.num_programs(0)
+    depth = shifted.shape[1]
     blocks = samples // LANES + 2 * EDGE
-
-    def sends(at, slot):
+    width = GROUP * LAG_WIDTH
+    half_of = LAG_BLOCKS // 2
+
+    def sends(pair, halves):
         return [
             pltpu.make_async_copy(
-                ready.at[slot, q].reshape(sources, GROUP, LANES),
-                out.at[:, pl.ds(at * GROUP, GROUP), pl.ds(q * LANES, LANES)],
-                sem.at[slot],
+                ready.at[m, q].reshape(sources, GROUP, LANES),
+                out.at[:, pl.ds((pair * UNITS + m) * GROUP, GROUP), pl.ds(q * LANES, LANES)],
+                sem.at[m, q],
             )
-            for q in range(LAG_BLOCKS)
+            for m in range(UNITS)
+            for q in halves
         ]
 
-    @pl.when(step == 0)
-    def _():
-        start = 0
-        for part in parts:
-            all_rows[start : start + part.shape[0], :] = part[...].astype(F32)
-            start += part.shape[0]
-        lines[blocks * sources :, :] = jnp.zeros((sources, LANES), F32)
-
-        for s in range(sources):
-            lines[pl.ds(s, blocks, stride=sources), :] = all_rows[
-                pl.ds(place[s], blocks, stride=MAX_OWN), :
-            ]
-
-        lane = lax.broadcasted_iota(jnp.int32, (sources, LANES), 1)
-        for p in range(PIECES):
-            turn = p * LAG_WIDTH
-            turned = None
-            for b in range(blocks + 1):
-                line = lines[b * sources : (b + 1) * sources, :]
-                following = pltpu.roll(line, LANES - turn, 1) if p else line
-                if b:
-                    block = b - 1
-                    value = jnp.where(lane < LANES - turn, turned, following).astype(BF16)
-                    for q in range(LAG_BLOCKS):
-                        if 0 <= block - q < depth // LANES:
-                            at = (q * PIECES + p) * sources
-                            windows[at : at + sources, (block - q) * LANES : (block - q + 1) * LANES] = value
-                turned = following
-
-    @pl.when(step >= 2)
-    def _():
-        for copy in sends(step - 2, slot):
-            copy.wait()
-
-    width = GROUP * LAG_WIDTH
-    result = dot_t(windows[...], shifted[pl.ds(pl.multiple_of(step * width, width), width), :])
     lane = lax.broadcasted_iota(jnp.int32, (sources, LANES), 1)
-    for q in range(LAG_BLOCKS):
+
+    def arrange(m, q):
+        whole = [pltpu.matmul_pop(sums[m][q * PIECES + p]) for p in range(PIECES)]
         for half in range(width // LANES):
-            tiles = [
-                result[
-                    (q * PIECES + p) * sources : (q * PIECES + p + 1) * sources,
-                    half * LANES : (half + 1) * LANES,
-                ]
-                * scale
-                for p in range(PIECES)
-            ]
+            tiles = [piece[:, half * LANES : (half + 1) * LANES] * scale for piece in whole]
             gap = PIECES // 2
             while gap:
                 wide = gap * LAG_WIDTH
@@ -201,15 +181,88 @@
                     tiles[p + gap] = jnp.where(low_half, pltpu.roll(a, LANES - wide, 1), b)
                 gap //= 2
             for p in range(PIECES):
-                ready.at[slot, q][pl.ds(half * PIECES + p, sources, stride=GROUP), :] = tiles[p]
-    for copy in sends(step, slot):
+                ready.at[m, q][pl.ds(half * PIECES + p, sources, stride=GROUP), :] = tiles[p]
+
+    first, second = list(range(half_of)), list(range(half_of, LAG_BLOCKS))
+
+    def chunk(now, before):
+        todo = [(m, q) for q in before for m in range(UNITS)]
+        count = depth // TILE
+        for k in range(count):
+            for m in range(UNITS):
+                at = pl.multiple_of((step * UNITS + m) * width, width)
+                pltpu.matmul_push_rhs(
+                    shifted[pl.ds(at, width), k * TILE : (k + 1) * TILE], k % 2, m, transpose=True
+                )
+            for i, t in enumerate(range(now[0] * PIECES, (now[-1] + 1) * PIECES)):
+                left = windows[t * sources : (t + 1) * sources, k * TILE : (k + 1) * TILE]
+                for m in range(UNITS):
+                    pltpu.matmul_acc_lhs(sums[m][t], left, load_staged_rhs=k % 2 if i == 0 else None)
+            if k % 2 and todo:
+                arrange(*todo.pop(0))
+        while todo:
+            arrange(*todo.pop(0))
+
+    @pl.when(step == 0)
+    def _():
+        start = 0
+        for part in parts:
+            all_rows[start : start + part.shape[0], :] = part[...].astype(F32)
+            start += part.shape[0]
+        lines[blocks * sources :, :] = jnp.zeros((sources, LANES), F32)
+        windows[:, samples + LANES :] = jnp.zeros((windows.shape[0], depth - samples - LANES), BF16)
+
+        for s in range(sources):
+            lines[pl.ds(s, blocks, stride=sources), :] = all_rows[
+                pl.ds(place[s], blocks, stride=MAX_OWN), :
+            ]
+
+        for p in range(PIECES):
+            turn = p * LAG_WIDTH
+            turned = None
+            for b in range(blocks + 1):
+                line = lines[b * sources : (b + 1) * sources, :]
+                following = pltpu.roll(line, LANES - turn, 1) if p else line
+                if b:
+                    block = b - 1
+                    value = jnp.where(lane < LANES - turn, turned, following).astype(BF16)
+                    for q in range(LAG_BLOCKS):
+                        if 0 <= block - q <= samples // LANES:
+                            at = (q * PIECES + p) * sources
+                            windows[at : at + sources, (block - q) * LANES : (block - q + 1) * LANES] = value
+                turned = following
+
+    @pl.when(step >= 2)
+    def _():
+        for copy in sends(step - 2, second):
+            copy.wait()
+
+    chunk(first, second)
+
+    @pl.when(step >= 1)
+    def _():
+        for copy in sends(step - 1, second):
+            copy.start()
+        for copy in sends(step - 1, first):
+            copy.wait()
+
+    chunk(second, first)
+    for copy in sends(step, first):
         copy.start()
 
-    @pl.when(step == pl.num_programs(0) - 1)
+    @pl.when(step == steps - 1)
     def _():
-        for copy in sends(step - 1, 1 - slot):
-            copy.wait()
-        for copy in sends(step, slot):
+        @pl.when(step >= 1)
+        def _():
+            for copy in sends(step - 1, second):
+                copy.wait()
+
+        for q in second:
+            for m in range(UNITS):
+                arrange(m, q)
+        for copy in sends(step, second):
+            copy.start()
+        for copy in sends(step, first) + sends(step, second):
             copy.wait()
 
 
@@ -237,7 +290,7 @@
         functools.partial(shifted_kernel, fir_taps=fir_taps),
         in_specs=[SMEM] + [VMEM] * 4,
         out_specs=VMEM,
-        out_shape=jax.ShapeDtypeStruct((channels * LAG_WIDTH, samples + LANES), BF16),
+        out_shape=jax.ShapeDtypeStruct((channels * LAG_WIDTH, -(-(samples + LANES) // TILE) * TILE), BF16),
         scratch_shapes=[pltpu.VMEM((channels * samples // LANES, LANES), F32)],
         compiler_params=pltpu.CompilerParams(vmem_limit_bytes=32 * MIB),
         cost_estimate=pl.CostEstimate(
@@ -260,18 +313,18 @@
             pieces=len(parts),
             scale=scale,
         ),
-        grid=(channels // GROUP,),
+        grid=(channels // (UNITS * GROUP),),
         in_specs=[SMEM] + [VMEM] * len(parts) + [VMEM],
         out_specs=pl.BlockSpec(memory_space=pl.ANY),
         out_shape=jax.ShapeDtypeStruct((sources, channels, 2 * LAG_HALF), F32),
         scratch_shapes=[
             pltpu.VMEM((rows, LANES), F32),
             pltpu.VMEM(((blocks + 1) * sources, LANES), F32),
-            pltpu.VMEM((LAG_BLOCKS * PIECES * sources, samples + LANES), BF16),
-            pltpu.VMEM((2, LAG_BLOCKS, sources * GROUP, LANES), F32),
-            pltpu.SemaphoreType.DMA((2,)),
+            pltpu.VMEM((LAG_BLOCKS * PIECES * sources, shifted.shape[1]), BF16),
+            pltpu.VMEM((UNITS, LAG_BLOCKS, sources * GROUP, LANES), F32),
+            pltpu.SemaphoreType.DMA((UNITS, LAG_BLOCKS)),
         ],
-        compiler_params=pltpu.CompilerParams(vmem_limit_bytes=48 * MIB),
+        compiler_params=pltpu.CompilerParams(vmem_limit_bytes=24 * MIB),
         name="correlate",
     )(place, *parts, shifted)
 

time: 65.3 us -> 49.5 us (0.76)
  Pallas kernels: 36.2 us -> 24.6 us
  local copies, waits for them, and re-layouts: 8.11 us -> 3.91 us
    pallas_call x1, Pallas kernels: 24.1 us -> 17.5 us  [correlate(): pl.pallas_call(functools.partial(correlate_kernel, sources=sources, chann...]
    pallas_call x1, Pallas kernels: 10.8 us -> 5.77 us  [shifted_rows(): pl.pallas_call(functools.partial(shifted_kernel, fir_taps=fir_taps), in_s...]
    unnamed x8 -> x6, local copies, waits for them, and re-layouts: 6.38 us -> 2.19 us
  transfers between devices with their start and end apart: 7 -> 7, of which waited for: 1 -> 1; matrix products, arithmetic and copies ran while one was open for 4% -> 5% of each run, Pallas kernels for 17% -> 12%
where the time goes in v2:
time: 49.5 us; the launch traced here: 49.2 us
  Pallas kernels  24.6 us (50%)
  starting transfers between devices  12.1 us (24%)
  waiting for transfers between devices  6.81 us (14%)
  local copies, waits for them, and re-layouts  3.91 us (8%)
  other arithmetic  1.72 us (3%)
    pallas_call x1, Pallas kernels, correlate(): pl.pallas_call(functools.partial(correlate_kernel, sources=sources, chann...  17.5 us
    ppermute x5, starting transfers between devices, swap(): lax.ppermute(value, 'chan', [(i, i ^ distance) for i in range(blocks_of)])  7.77 us
    ppermute x5, waiting for transfers between devices, swap(): lax.ppermute(value, 'chan', [(i, i ^ distance) for i in range(blocks_of)])  6.8 us
    pallas_call x1, Pallas kernels, shifted_rows(): pl.pallas_call(functools.partial(shifted_kernel, fir_taps=fir_taps), in_s...  5.77 us
    ppermute x1, starting transfers between devices, body(): low = lax.ppermute(traces[:, samples - width:], 'tm', forward)  3.04 us
    unnamed x6, local copies, waits for them, and re-layouts  2.19 us
    ppermute x1, starting transfers between devices, body(): high = lax.ppermute(traces[:, :width], 'tm', [(b, a) for a, b in forward])  1.29 us
    pallas_call x1, Pallas kernels, source_rows(): pl.pallas_call(functools.partial(source_kernel, fir_taps=fir_taps), in_sp...  1.29 us
  transfers between devices with their start and end apart: 7, of which 1 were waited for; matrix products, arithmetic and copies ran while one was open for 5% of the time, Pallas kernels for 12%

profile of v2, /device:TPU:0, one launch (start us, length us, event | category | flops | bytes accessed | tf_op | source)
XLA Modules:
  0.0 49.2 jit_solution(15752671270650037656)
XLA Ops:
  0.0 1.0 %fusion.6 = (f32[80,384]{1,0:T(8,128)S(1)}, f32[80,384]{1,0:T(8,128)S(1)}) fusion(f32[80,2048]{1,0:T(8,128)} %traces.3), kind=kLoop, calls=%fused_computation.23 | loop fusion | bytes 491520 | tf_op jit(solution)/shard_map/slice | solution.py:340
  1.0 1.3 %collective-permute-start.1 = (f32[80,384]{1,0:T(8,128)S(1)}, f32[80,384]{1,0:T(8,128)S(1)}, u32[]{:S(2)}, u32[]{:S(2)}) collective-permute-start(f32[80,384]{1,0:T(8,128)S(1)} %get-tuple-element.7), channel_id=1, source_target_pairs={{1,0},{2,1},{3,2},{5,4},{6,5},{7,6},{9,8},{10,9},{11,10},{13,12},{... | collective-permute-start | bytes 368648 | tf_op jit(solution)/shard_map/ppermute | solution.py:340
  2.3 3.0 %collective-permute-start = (f32[80,384]{1,0:T(8,128)S(1)}, f32[80,384]{1,0:T(8,128)S(1)}, u32[]{:S(2)}, u32[]{:S(2)}) collective-permute-start(f32[80,384]{1,0:T(8,128)S(1)} %get-tuple-element.8), channel_id=1, source_target_pairs={{0,1},{1,2},{2,3},{4,5},{5,6},{6,7},{8,9},{9,10},{10,11},{12,13},{... | collective-permute-start | bytes 368648 | tf_op jit(solution)/shard_map/ppermute | solution.py:339
  5.3 0.7 %broadcast_compare_fusion = (pred[64]{0:T(512)(128)(4,1)S(1)}, s32[64]{0:T(128)S(1)}) fusion(s32[]{:T(128)S(6)} %axis_index.23, s32[64]{0:T(128)} %param.5), kind=kLoop, calls=%fused_computation.22 | loop fusion | flops 576 | bytes 580 | tf_op jit(solution)/shard_map/eq | solution.py:349
  6.0 0.2 convert_reduce_fusion
  6.2 0.7 %multiply_subtract_fusion = (s32[64]{0:T(128)S(1)}, s32[64]{0:T(128)S(1)}) fusion(s32[64]{0:T(128)} %param.5, s32[64]{0:T(128)S(1)} %get-tuple-element.6, s32[64]{0:T(128)S(1)} %convert_reduce_fusion, s32[]{:T(128)S(6)} %axis_index.23), kind=kLoop, calls=%fused_computation.21 | loop fusion | flops 1856 | bytes 1284 | tf_op jit(solution)/shard_map/sub | solution.py:345
  6.9 0.1 pad_add_fusion.place
  6.9 0.7 %pad.4 = f32[384]{0:T(512)S(1)} pad(f32[65]{0:T(128)} %param.4, f32[]{:T(128)} %constant.52.clone.1), padding=96_223 | pad | bytes 1800 | tf_op jit(solution)/shard_map/jit(_pad)/pad | solution.py:353
  7.7 0.1 select_reduce_fusion.offset
  7.8 0.0 collective-permute-done.1.high
  7.8 0.0 collective-permute-done.low
  7.8 0.0 copy-start
  7.8 1.1 %copy-done = f32[80,2048]{1,0:T(8,128)S(1)} copy-done((f32[80,2048]{1,0:T(8,128)S(1)}, f32[80,2048]{1,0:T(8,128)}, u32[]{:S(2)}) %copy-start) | copy-done | bytes 655384
  8.9 1.3 %source_rows.1.refs_1_ = bf16[240,128]{1,0:T(8,128)(2,1)S(1)} custom-call(s32[12]{0:T(128)S(1)} %select_reduce_fusion.offset, s32[2]{0:T(128)S(1)} %pad_add_fusion.place, f32[80,2048]{1,0:T(8,128)S(1)} %copy-done, f32[80,384]{1,0:T(8,128)S(1)} %collective-permute-done.low, f32[80,384]{1,0:T(8,128)S(1)} %collective-permute-done.1.high, ...), custom_call_target="tpu_custom_call" | custom-call | tf_op jit(solution)/shard_map/source_rows/pallas_call | solution.py:276
  10.2 3.1 %collective-permute-start.3 = (bf16[240,128]{1,0:T(8,128)(2,1)S(1)}, bf16[240,128]{1,0:T(8,128)(2,1)S(1)}, u32[]{:S(2)}, u32[]{:S(2)}) collective-permute-start(bf16[240,128]{1,0:T(8,128)(2,1)S(1)} %source_rows.1.refs_1_), channel_id=1, source_target_pairs={{0,8},{4,12},{8,0},{12,4},{16,24},{20,28},{24,16},{28,20},{1,9},{5... | collective-permute-start | bytes 184328 | tf_op jit(solution)/shard_map/ppermute | solution.py:359
  13.3 2.5 %collective-permute-start.5 = (bf16[240,128]{1,0:T(8,128)(2,1)S(1)}, bf16[240,128]{1,0:T(8,128)(2,1)S(1)}, u32[]{:S(2)}, u32[]{:S(2)}) collective-permute-start(bf16[240,128]{1,0:T(8,128)(2,1)S(1)} %source_rows.1.refs_1_), channel_id=1, source_target_pairs={{0,24},{4,28},{8,16},{12,20},{16,8},{20,12},{24,0},{28,4},{1,25},{... | collective-permute-start | bytes 184328 | tf_op jit(solution)/shard_map/ppermute | solution.py:359
  15.8 0.1 collective-permute-start.4
  15.9 0.0 collective-permute-done.3
  15.9 6.8 %collective-permute-done.4 = bf16[240,128]{1,0:T(8,128)(2,1)S(1)} collective-permute-done((bf16[240,128]{1,0:T(8,128)(2,1)S(1)}, bf16[240,128]{1,0:T(8,128)(2,1)S(1)}, u32[]{:S(2)}, u32[]{:S(2)}) %collective-permute-start.4) | collective-permute-done | bytes 61472 | tf_op jit(solution)/shard_map/ppermute | solution.py:359
  22.7 0.0 collective-permute-done.5
  22.7 1.6 %collective-permute-start.6 = (bf16[720,128]{1,0:T(8,128)(2,1)S(1)}, bf16[720,128]{1,0:T(8,128)(2,1)S(1)}, u32[]{:S(2)}, u32[]{:S(2)}) collective-permute-start(bf16[720,128]{1,0:T(8,128)(2,1)S(1)} %constant_dynamic-update-slice_fusion.refs_3_), channel_id=1, source_target_pairs={{0,4},{4,0},{8,12},{12,8},{16,20},{20,16},{24,28},{28,24},{1,5},{5... | collective-permute-start | bytes 552968 | tf_op jit(solution)/shard_map/ppermute | solution.py:359
  24.3 0.5 %collective-permute-start.2 = (bf16[240,128]{1,0:T(8,128)(2,1)S(1)}, bf16[240,128]{1,0:T(8,128)(2,1)S(1)}, u32[]{:S(2)}, u32[]{:S(2)}) collective-permute-start(bf16[240,128]{1,0:T(8,128)(2,1)S(1)} %source_rows.1.refs_1_), channel_id=1, source_target_pairs={{0,4},{4,0},{8,12},{12,8},{16,20},{20,16},{24,28},{28,24},{1,5},{5... | collective-permute-start | bytes 184328 | tf_op jit(solution)/shard_map/ppermute | solution.py:359
  24.8 0.0 copy-start.1
  24.8 1.1 %copy-done.1 = f32[80,2048]{1,0:T(8,128)S(1)} copy-done((f32[80,2048]{1,0:T(8,128)S(1)}, f32[80,2048]{1,0:T(8,128)}, u32[]{:S(2)}) %copy-start.1) | copy-done | bytes 655384
  25.9 5.8 %shifted_rows.1.refs_5_ = bf16[2560,2304]{1,0:T(8,128)(2,1)S(1)} custom-call(s32[2]{0:T(128)S(1)} %pad_add_fusion.place, f32[80,2048]{1,0:T(8,128)S(1)} %copy-done.1, f32[80,384]{1,0:T(8,128)S(1)} %collective-permute-done.low, f32[80,384]{1,0:T(8,128)S(1)} %collective-permute-done.1.high, f32[1,384]{1,0:T(1,128)S(1)} %broadcast_in_dim.28.taps_row), custom_call_target="tpu_custom_call" | custom-call | flops 377487360 | bytes 3276800 | tf_op jit(solution)/shard_map/shifted_rows/pallas_call | solution.py:289
  31.7 0.0 collective-permute-done.2.refs_2_
  31.7 0.0 collective-permute-done.6.refs_4_
  31.7 17.5 %correlate.1 = f32[64,80,512]{2,1,0:T(8,128)} custom-call(s32[64]{0:T(128)S(1)} %get-tuple-element.10.refs_0_, bf16[240,128]{1,0:T(8,128)(2,1)S(1)} %source_rows.1.refs_1_, bf16[240,128]{1,0:T(8,128)(2,1)S(1)} %collective-permute-done.2.refs_2_, bf16[720,128]{1,0:T(8,128)(2,1)S(1)} %constant_dynamic-update-slice_fusion.refs_3_, ...), custom_call_target="tpu_custom_call" | custom-call | tf_op jit(solution)/shard_map/correlate/pallas_call | solution.py:307
  (4 shorter events, 0.0 us)
Async XLA Ops:
  1.0 6.8 %collective-permute-start.1 = (f32[80,384]{1,0:T(8,128)S(1)}, f32[80,384]{1,0:T(8,128)S(1)}, u32[]{:S(2)}, u32[]{:S(2)}) collective-permute-start(f32[80,384]{1,0:T(8,128)S(1)} %get-tuple-element.7), channel_id=1, source_target_pairs={{1,0},{2,1},{3,2},{5,4},{6,5},{7,6},{9,8},{10,9},{11,10},{13,12},{... | collective-permute-start | bytes 368648 | tf_op jit(solution)/shard_map/ppermute | solution.py:340
  2.3 5.5 %collective-permute-start = (f32[80,384]{1,0:T(8,128)S(1)}, f32[80,384]{1,0:T(8,128)S(1)}, u32[]{:S(2)}, u32[]{:S(2)}) collective-permute-start(f32[80,384]{1,0:T(8,128)S(1)} %get-tuple-element.8), channel_id=1, source_target_pairs={{0,1},{1,2},{2,3},{4,5},{5,6},{6,7},{8,9},{9,10},{10,11},{12,13},{... | collective-permute-start | bytes 368648 | tf_op jit(solution)/shard_map/ppermute | solution.py:339
  7.8 1.1 %copy-start = (f32[80,2048]{1,0:T(8,128)S(1)}, f32[80,2048]{1,0:T(8,128)}, u32[]{:S(2)}) copy-start(f32[80,2048]{1,0:T(8,128)} %traces.3) | copy-start | bytes 1966084
  10.2 5.7 %collective-permute-start.3 = (bf16[240,128]{1,0:T(8,128)(2,1)S(1)}, bf16[240,128]{1,0:T(8,128)(2,1)S(1)}, u32[]{:S(2)}, u32[]{:S(2)}) collective-permute-start(bf16[240,128]{1,0:T(8,128)(2,1)S(1)} %source_rows.1.refs_1_), channel_id=1, source_target_pairs={{0,8},{4,12},{8,0},{12,4},{16,24},{20,28},{24,16},{28,20},{1,9},{5... | collective-permute-start | bytes 184328 | tf_op jit(solution)/shard_map/ppermute | solution.py:359
  13.3 9.4 %collective-permute-start.5 = (bf16[240,128]{1,0:T(8,128)(2,1)S(1)}, bf16[240,128]{1,0:T(8,128)(2,1)S(1)}, u32[]{:S(2)}, u32[]{:S(2)}) collective-permute-start(bf16[240,128]{1,0:T(8,128)(2,1)S(1)} %source_rows.1.refs_1_), channel_id=1, source_target_pairs={{0,24},{4,28},{8,16},{12,20},{16,8},{20,12},{24,0},{28,4},{1,25},{... | collective-permute-start | bytes 184328 | tf_op jit(solution)/shard_map/ppermute | solution.py:359
  15.8 6.9 %collective-permute-start.4 = (bf16[240,128]{1,0:T(8,128)(2,1)S(1)}, bf16[240,128]{1,0:T(8,128)(2,1)S(1)}, u32[]{:S(2)}, u32[]{:S(2)}) collective-permute-start(bf16[240,128]{1,0:T(8,128)(2,1)S(1)} %source_rows.1.refs_1_), channel_id=1, source_target_pairs={{0,16},{4,20},{8,24},{12,28},{16,0},{20,4},{24,8},{28,12},{1,17},{... | collective-permute-start | bytes 184328 | tf_op jit(solution)/shard_map/ppermute | solution.py:359
  22.7 9.0 %collective-permute-start.6 = (bf16[720,128]{1,0:T(8,128)(2,1)S(1)}, bf16[720,128]{1,0:T(8,128)(2,1)S(1)}, u32[]{:S(2)}, u32[]{:S(2)}) collective-permute-start(bf16[720,128]{1,0:T(8,128)(2,1)S(1)} %constant_dynamic-update-slice_fusion.refs_3_), channel_id=1, source_target_pairs={{0,4},{4,0},{8,12},{12,8},{16,20},{20,16},{24,28},{28,24},{1,5},{5... | collective-permute-start | bytes 552968 | tf_op jit(solution)/shard_map/ppermute | solution.py:359
  24.3 7.4 %collective-permute-start.2 = (bf16[240,128]{1,0:T(8,128)(2,1)S(1)}, bf16[240,128]{1,0:T(8,128)(2,1)S(1)}, u32[]{:S(2)}, u32[]{:S(2)}) collective-permute-start(bf16[240,128]{1,0:T(8,128)(2,1)S(1)} %source_rows.1.refs_1_), channel_id=1, source_target_pairs={{0,4},{4,0},{8,12},{12,8},{16,20},{20,16},{24,28},{28,24},{1,5},{5... | collective-permute-start | bytes 184328 | tf_op jit(solution)/shard_map/ppermute | solution.py:359
  24.8 1.1 %copy-start.1 = (f32[80,2048]{1,0:T(8,128)S(1)}, f32[80,2048]{1,0:T(8,128)}, u32[]{:S(2)}) copy-start(f32[80,2048]{1,0:T(8,128)} %traces.3) | copy-start | bytes 1966084

commit v3 on v2

v3 whole, which is shorter than its diff:
```python
import functools
import math

import jax
import jax.numpy as jnp
from jax import lax
from jax.experimental import pallas as pl
from jax.experimental.pallas import tpu as pltpu
from jax.sharding import PartitionSpec as P

LAG_HALF = 256
NORM_HALF = 64
MAX_OWN = 12
EPSILON = 1e-05

LANES = 128
LAG_WIDTH = 32
PIECES = LANES // LAG_WIDTH
LAG_BLOCKS = 2 * LAG_HALF // LANES
SIDE = 3
EDGE = LAG_HALF // LANES
ROWS = 16
GROUP = 8
TILE = 256
UNITS = 2
EARLY = (1,)
MIB = 2**20
F32 = jnp.float32
BF16 = jnp.bfloat16


def split(value):
    high = value.astype(BF16)
    return high, (value - high.astype(F32)).astype(BF16)


def dot_t(left, right):
    return lax.dot_general(left, right, (((1,), (1,)), ((), ())), preferred_element_type=F32)


def stacked(blocks):
    wide = [
        jnp.concatenate([blocks[b - 1], blocks[b], blocks[b + 1]], axis=1)
        for b in range(1, len(blocks) - 1)
    ]
    return jnp.concatenate(wide, axis=0)


def normalize(pairs, first, last, has_low, has_high, taps_row):
    rows = pairs[0][0].shape[0]
    row = lax.broadcasted_iota(jnp.int32, (LANES, 3 * LANES), 0)
    lane = lax.broadcasted_iota(jnp.int32, (LANES, 3 * LANES), 1)
    toeplitz = pltpu.roll(jnp.broadcast_to(taps_row, (LANES, 3 * LANES)), 0, 1, stride=1, stride_axis=0)
    taps_high, taps_low = split(toeplitz)
    reach = lane - row - (LANES - NORM_HALF)
    band = jnp.where((reach >= 0) & (reach <= 2 * NORM_HALF), 1.0, 0.0).astype(BF16)
    wide_high = stacked([p[0] for p in pairs])
    wide_low = stacked([p[1] for p in pairs])
    filtered = dot_t(wide_high, taps_high) + dot_t(wide_low, taps_high) + dot_t(wide_high, taps_low)
    inner = []
    for k in range(len(pairs) - 2):
        block = filtered[k * rows : (k + 1) * rows]
        number = first + 1 + k
        if number < 0:
            block = jnp.where(has_low, block, 0.0)
        elif number > last:
            block = jnp.where(has_high, block, 0.0)
        inner.append(block)
    sizes = [split(jnp.abs(block)) for block in inner]
    total = dot_t(stacked([p[0] for p in sizes]), band) + dot_t(stacked([p[1] for p in sizes]), band)
    level = total / (2 * NORM_HALF + 1)
    return [
        block / (EPSILON + level[k * rows : (k + 1) * rows]) for k, block in enumerate(inner[1:-1])
    ]


def dot(left, right):
    return jnp.dot(left, right, preferred_element_type=F32)


def pick_kernel(place, index, traces, pick, high, low, rows_high, rows_low):
    channels = traces.shape[0]
    sources = index.shape[1]
    channel = lax.broadcasted_iota(jnp.int32, (channels, sources), 0) + place[3] * channels
    number = lax.broadcasted_iota(jnp.int32, (channels, sources), 1).astype(F32)
    equal = jnp.where(index[...] == channel, 1.0, 0.0)
    here = jnp.sum(equal, axis=1, keepdims=True)
    order = jnp.sum(equal * number, axis=1, keepdims=True)
    across = lax.broadcasted_iota(jnp.int32, (ROWS, sources), 1).astype(F32).astype(BF16)
    here_row = dot_t(jnp.ones((ROWS, sources), BF16), equal.astype(BF16))
    order_row = dot_t(across, equal.astype(BF16))
    rank = jnp.sum(jnp.where(order < order_row[:1], here, 0.0), axis=0, keepdims=True)
    slot = lax.broadcasted_iota(jnp.int32, (ROWS, channels), 0).astype(F32)
    chosen = jnp.where((rank == slot) & (here_row > 0.5), 1.0, 0.0).astype(BF16)
    pick[...] = chosen
    first, second = split(traces[...])
    high[...] = first
    low[...] = second
    rows_high[...] = dot(chosen, first).astype(BF16)
    rows_low[...] = dot(chosen, second).astype(BF16)


def neighbours(place, a, b):
    even = place[2] == 0
    low = jnp.where(place[0] > 0, jnp.where(even, b, a), 0.0)
    high = jnp.where(place[0] < place[1] - 1, jnp.where(even, a, b), 0.0)
    return low, high


def source_kernel(place, pick, rows_high, rows_low, got_a, got_b, taps_row, out):
    own = rows_high.shape[1] // LANES

    def blocks_of(high, low, count):
        return [
            (high[:, b * LANES : (b + 1) * LANES], low[:, b * LANES : (b + 1) * LANES])
            for b in range(count)
        ]

    sides = []
    for edge in neighbours(place, got_a[...], got_b[...]):
        high, low = [dot(pick[...], part).astype(BF16) for part in split(edge)]
        sides.append(blocks_of(high, low, SIDE))
    nothing = jnp.zeros((ROWS, LANES), BF16)
    pairs = [(nothing, nothing)] + sides[0] + blocks_of(rows_high, rows_low, own) + sides[1]
    pairs += [(nothing, nothing)]
    normed = normalize(
        pairs, -SIDE - 1, own - 1, place[0] > 0, place[0] < place[1] - 1, taps_row[...]
    )
    packed = jnp.concatenate([block[:MAX_OWN] for block in normed], axis=0)
    out[...] = packed.astype(BF16)


def normed_kernel(place, index, high, low, got_a, got_b, taps_row, out, start, *, owners, paired):
    channels, samples = high.shape
    own = samples // LANES
    sources = index.shape[1]
    line = jnp.broadcast_to(index[...], (sources, sources))
    ahead = lax.broadcasted_iota(jnp.int32, (sources, sources), 0)
    behind = lax.broadcasted_iota(jnp.int32, (sources, sources), 1)

    def owner_of(value):
        return ((value.astype(F32) + 0.5) * (1.0 / channels)).astype(jnp.int32)

    upright = jnp.sum(jnp.where(ahead == behind, line, 0).astype(F32), axis=1, keepdims=True)
    owner = owner_of(index[...])
    same = (owner_of(upright) == owner) & (ahead < behind)
    rank = jnp.sum(jnp.where(same, 1.0, 0.0), axis=0, keepdims=True).astype(jnp.int32)
    if paired:
        apart = owner ^ place[3]
        piece = lax.shift_right_logical(apart, 1) + (apart & 1) * (owners // 2)
    else:
        piece = owner
    start[...] = piece * (MAX_OWN * (own + 2 * EDGE)) + rank
    before, after = neighbours(place, got_a[...], got_b[...])
    nothing = jnp.zeros((channels, LANES), BF16)
    pairs = [(nothing, nothing), split(before[:, (SIDE - 1) * LANES :])]
    pairs += [
        (high[:, b * LANES : (b + 1) * LANES], low[:, b * LANES : (b + 1) * LANES]) for b in range(own)
    ]
    pairs += [split(after[:, :LANES]), (nothing, nothing)]
    normed = normalize(pairs, -2, own - 1, place[0] > 0, place[0] < place[1] - 1, taps_row[...])
    for b, block in enumerate(normed):
        out[b * channels : (b + 1) * channels, :] = block


def shifted_kernel(normed, out, *, channels):
    own = normed.shape[0] // channels
    lane = lax.broadcasted_iota(jnp.int32, (LAG_WIDTH, LANES), 1)
    later = lane >= lax.broadcasted_iota(jnp.int32, (LAG_WIDTH, LANES), 0)
    beyond = (own + 1) * LANES
    if out.shape[1] > beyond:
        out[:, beyond:] = jnp.zeros((out.shape[0], out.shape[1] - beyond), BF16)

    @pl.loop(0, channels, unroll=8)
    def _(c):
        before = jnp.zeros((LAG_WIDTH, LANES), F32)
        at = pl.multiple_of(c * LAG_WIDTH, LAG_WIDTH)
        for b in range(own + 1):
            if b < own:
                line = normed[pl.ds(b * channels + c, 1), :]
                turned = pltpu.roll(
                    jnp.broadcast_to(line, (LAG_WIDTH, LANES)), 0, 1, stride=1, stride_axis=0
                )
            else:
                turned = jnp.zeros((LAG_WIDTH, LANES), F32)
            out[pl.ds(at, LAG_WIDTH), b * LANES : (b + 1) * LANES] = jnp.where(
                later, turned, before
            ).astype(BF16)
            before = turned


def correlate_kernel(*refs, sources, **sizes):
    tiles_of = LAG_BLOCKS * PIECES

    def run(*sums):
        split_sums = [sums[m * tiles_of : (m + 1) * tiles_of] for m in range(UNITS)]
        correlate_steps(split_sums, *refs, sources=sources, **sizes)

    pl.run_scoped(
        run, *[pltpu.ACC(m)((sources, TILE), F32) for m in range(UNITS) for _ in range(tiles_of)]
    )


def correlate_steps(sums, place, *refs, sources, channels, samples, pieces, scale):
    parts = refs[:pieces]
    shifted, out, all_rows, lines, windows, ready, sem = refs[pieces:]
    step = pl.program_id(0)
    steps = pl.num_programs(0)
    depth = shifted.shape[1]
    blocks = samples // LANES + 2 * EDGE
    width = GROUP * LAG_WIDTH
    half_of = LAG_BLOCKS // 2

    boxes = ready.reshape(sources, UNITS + 1, LAG_BLOCKS + 1, GROUP, LANES)
    spread = (UNITS + 1) * (LAG_BLOCKS + 1) * GROUP

    def send(pair, halves):
        return pltpu.make_async_copy(
            boxes.at[:, 0:UNITS, halves[0] : halves[-1] + 1],
            out.at[:, pl.ds(pair * UNITS, UNITS), halves[0] : halves[-1] + 1],
            sem.at[halves[0] // half_of],
        )

    lane = lax.broadcasted_iota(jnp.int32, (sources, LANES), 1)

    def arrange(m, q):
        whole = [pltpu.matmul_pop(sums[m][q * PIECES + p]) for p in range(PIECES)]
        for half in range(width // LANES):
            tiles = [piece[:, half * LANES : (half + 1) * LANES] * scale for piece in whole]
            gap = PIECES // 2
            while gap:
                wide = gap * LAG_WIDTH
                low_half = lax.rem(lane, 2 * wide) < wide
                for p in range(PIECES):
                    if p & gap:
                        continue
                    a, b = tiles[p], tiles[p + gap]
                    tiles[p] = jnp.where(low_half, a, pltpu.roll(b, wide, 1))
                    tiles[p + gap] = jnp.where(low_half, pltpu.roll(a, LANES - wide, 1), b)
                gap //= 2
            for p in range(PIECES):
                at = (m * (LAG_BLOCKS + 1) + q) * GROUP + half * PIECES + p
                ready[pl.ds(at, sources, stride=spread), :] = tiles[p]

    first, second = list(range(half_of)), list(range(half_of, LAG_BLOCKS))

    def chunk(now, before):
        todo = [(m, q) for q in before for m in range(UNITS)]
        count = depth // TILE
        for k in range(count):
            for m in range(UNITS):
                at = pl.multiple_of((step * UNITS + m) * width, width)
                pltpu.matmul_push_rhs(
                    shifted[pl.ds(at, width), k * TILE : (k + 1) * TILE], k % 2, m, transpose=True
                )
            for i, t in enumerate(range(now[0] * PIECES, (now[-1] + 1) * PIECES)):
                left = windows[t * sources : (t + 1) * sources, k * TILE : (k + 1) * TILE]
                for m in range(UNITS):
                    pltpu.matmul_acc_lhs(sums[m][t], left, load_staged_rhs=k % 2 if i == 0 else None)
            if k % 2 and todo:
                arrange(*todo.pop(0))
        while todo:
            arrange(*todo.pop(0))

    @pl.when(step == 0)
    def _():
        start = 0
        for part in parts:
            all_rows[start : start + part.shape[0], :] = part[...].astype(F32)
            start += part.shape[0]
        lines[blocks * sources :, :] = jnp.zeros((sources, LANES), F32)
        windows[:, samples + LANES :] = jnp.zeros((windows.shape[0], depth - samples - LANES), BF16)

        for s in range(sources):
            lines[pl.ds(s, blocks, stride=sources), :] = all_rows[
                pl.ds(place[0, s], blocks, stride=MAX_OWN), :
            ]

        for p in range(PIECES):
            turn = p * LAG_WIDTH
            turned = None
            for b in range(blocks + 1):
                line = lines[b * sources : (b + 1) * sources, :]
                following = pltpu.roll(line, LANES - turn, 1) if p else line
                if b:
                    block = b - 1
                    value = jnp.where(lane < LANES - turn, turned, following).astype(BF16)
                    for q in range(LAG_BLOCKS):
                        if 0 <= block - q <= samples // LANES:
                            at = (q * PIECES + p) * sources
                            windows[at : at + sources, (block - q) * LANES : (block - q + 1) * LANES] = value
                turned = following

    @pl.when(step >= 2)
    def _():
        send(step - 2, second).wait()

    chunk(first, second)

    @pl.when(step >= 1)
    def _():
        send(step - 1, second).start()
        send(step - 1, first).wait()

    chunk(second, first)
    send(step, first).start()

    @pl.when(step == steps - 1)
    def _():
        @pl.when(step >= 1)
        def _():
            send(step - 1, second).wait()

        for q in second:
            for m in range(UNITS):
                arrange(m, q)
        send(step, second).start()
        send(step, first).wait()
        send(step, second).wait()


SMEM = pl.BlockSpec(memory_space=pltpu.SMEM)
VMEM = pl.BlockSpec(memory_space=pltpu.VMEM)


def picked_rows(place, index, traces):
    channels, samples = traces.shape
    slab = jax.ShapeDtypeStruct(traces.shape, BF16)
    rows = jax.ShapeDtypeStruct((ROWS, samples), BF16)
    return pl.pallas_call(
        pick_kernel,
        in_specs=[SMEM, VMEM, VMEM],
        out_specs=[VMEM] * 5,
        out_shape=[jax.ShapeDtypeStruct((ROWS, channels), BF16), slab, slab, rows, rows],
        compiler_params=pltpu.CompilerParams(vmem_limit_bytes=8 * MIB),
        name="picked_rows",
    )(place, index[None], traces)


def source_rows(place, pick, rows_high, rows_low, got_a, got_b, taps_row):
    blocks = rows_high.shape[1] // LANES + 2 * EDGE
    return pl.pallas_call(
        source_kernel,
        in_specs=[SMEM] + [VMEM] * 6,
        out_specs=VMEM,
        out_shape=jax.ShapeDtypeStruct((blocks * MAX_OWN, LANES), BF16),
        compiler_params=pltpu.CompilerParams(vmem_limit_bytes=8 * MIB),
        name="source_rows",
    )(place, pick, rows_high, rows_low, got_a, got_b, taps_row)


def normed_rows(place, index, high, low, got_a, got_b, taps_row, owners, paired):
    channels, samples = high.shape
    return pl.pallas_call(
        functools.partial(normed_kernel, owners=owners, paired=paired),
        in_specs=[SMEM] + [VMEM] * 6,
        out_specs=[VMEM] * 2,
        out_shape=[
            jax.ShapeDtypeStruct((channels * samples // LANES, LANES), F32),
            jax.ShapeDtypeStruct((1, index.shape[0]), jnp.int32),
        ],
        compiler_params=pltpu.CompilerParams(vmem_limit_bytes=24 * MIB),
        cost_estimate=pl.CostEstimate(
            flops=2 * 5 * channels * samples * 3 * LANES,
            bytes_accessed=16 * channels * samples,
            transcendentals=0,
        ),
        name="normed_rows",
    )(place, index[None], high, low, got_a, got_b, taps_row)


def shifted_rows(normed, channels):
    samples = normed.shape[0] // channels * LANES
    depth = -(-(samples + LANES) // TILE) * TILE
    return pl.pallas_call(
        functools.partial(shifted_kernel, channels=channels),
        in_specs=[VMEM],
        out_specs=VMEM,
        out_shape=jax.ShapeDtypeStruct((channels * LAG_WIDTH, depth), BF16),
        compiler_params=pltpu.CompilerParams(vmem_limit_bytes=4 * MIB),
        cost_estimate=pl.CostEstimate(
            flops=4 * channels * LAG_WIDTH * depth,
            bytes_accessed=2 * channels * LAG_WIDTH * depth,
            transcendentals=0,
        ),
        name="shifted_rows",
    )(normed)


def correlate(place, parts, shifted, sources, channels, samples):
    blocks = samples // LANES + 2 * EDGE
    rows = sum(part.shape[0] for part in parts)
    scale = 1.0 / math.sqrt(samples)
    boxes = pl.pallas_call(
        functools.partial(
            correlate_kernel,
            sources=sources,
            channels=channels,
            samples=samples,
            pieces=len(parts),
            scale=scale,
        ),
        grid=(channels // (UNITS * GROUP),),
        in_specs=[SMEM] + [VMEM] * len(parts) + [VMEM],
        out_specs=pl.BlockSpec(memory_space=pl.ANY),
        out_shape=jax.ShapeDtypeStruct(
            (sources, channels // GROUP, LAG_BLOCKS, GROUP, LANES), F32
        ),
        scratch_shapes=[
            pltpu.VMEM((rows, LANES), F32),
            pltpu.VMEM(((blocks + 1) * sources, LANES), F32),
            pltpu.VMEM((LAG_BLOCKS * PIECES * sources, shifted.shape[1]), BF16),
            pltpu.VMEM((sources * (UNITS + 1) * (LAG_BLOCKS + 1) * GROUP, LANES), F32),
            pltpu.SemaphoreType.DMA((2,)),
        ],
        compiler_params=pltpu.CompilerParams(vmem_limit_bytes=24 * MIB),
        name="correlate",
    )(place, *parts, shifted)
    return boxes.transpose(0, 1, 3, 2, 4).reshape(sources, channels, 2 * LAG_HALF)


def body(traces, fir_taps, source_index):
    channels, samples = traces.shape
    taps = fir_taps.shape[0]
    slabs = lax.axis_size("tm")
    owners = lax.axis_size("chan")
    slab = lax.axis_index("tm")
    in_pairs = slabs % 2 == 0
    parity = slab % 2 if in_pairs else 0 * slab
    place = jnp.stack([slab, jnp.full_like(slab, slabs), parity, lax.axis_index("chan")])
    place = place.astype(jnp.int32)
    lead = LANES - (taps - 1) // 2
    taps_row = jnp.pad(fir_taps, (lead, 3 * LANES - lead - taps))[None]

    left, right = traces[:, : SIDE * LANES], traces[:, samples - SIDE * LANES :]
    if in_pairs:
        edge_a, edge_b = jnp.where(parity == 0, right, left), jnp.where(parity == 0, left, right)
        got_b = lax.ppermute(edge_b, "tm", [(i, (i + 1 if i % 2 else i - 1) % slabs) for i in range(slabs)])
        got_a = lax.ppermute(edge_a, "tm", [(i, i ^ 1) for i in range(slabs)])
    else:
        got_b = lax.ppermute(right, "tm", [(i, i + 1) for i in range(slabs - 1)])
        got_a = lax.ppermute(left, "tm", [(i + 1, i) for i in range(slabs - 1)])
    pick, high, low, *rows = picked_rows(place, source_index, traces)
    own = source_rows(place, pick, *rows, got_a, got_b, taps_row)
    paired = owners in (4, 8)
    normed, start = normed_rows(
        place, source_index, high, low, got_a, got_b, taps_row, owners, paired
    )
    if paired:

        def swap(value, distance):
            return lax.ppermute(value, "chan", [(i, i ^ distance) for i in range(owners)])

        early = [swap(own, distance) for distance in EARLY]
        column = [swap(own, distance) for distance in range(2, owners, 2)]
        held = lax.optimization_barrier((*column, *early, normed))
        column, early, normed = list(held[: len(column)]), list(held[len(column) : -1]), held[-1]
        column = [own] + column
        late = jnp.concatenate(column[len(EARLY) :], axis=0)
        parts = column[: len(EARLY)] + [late] + early + [swap(late, 1)]
    else:
        parts = [lax.all_gather(own, "chan", axis=0, tiled=True)]
    shifted = shifted_rows(normed, channels)
    return correlate(start, parts, shifted, source_index.shape[0], channels, samples)[None]


def solution(mesh):
    placed = (P("chan", "tm"), P(), P())
    return jax.shard_map(
        body, mesh=mesh, in_specs=placed, out_specs=P("tm", None, "chan", None), check_vma=False
    )
```

time: 49.5 us -> 43.5 us (0.88)
  waiting for transfers between devices: 6.81 us -> 3.76 us
  starting transfers between devices: 12.1 us -> 10.1 us
  local copies, waits for them, and re-layouts: 3.91 us -> 3.16 us
  other arithmetic: 1.72 us -> 1.06 us
  Pallas kernels: 24.6 us -> 25.1 us
    ppermute x7, waiting for transfers between devices: 6.81 us -> 3.76 us  [the longest x5 3.75 us: swap(): lax.ppermute(value, 'chan', [(i, i ^ distance) for i in range(owners)])]
    ppermute x7, starting transfers between devices: 12.1 us -> 10.1 us  [the longest x5 6.95 us: swap(): lax.ppermute(value, 'chan', [(i, i ^ distance) for i in range(owners)])]
    select_n x0 -> x1, other arithmetic: none -> 0.98 us  [body(): jnp.where(parity == 0, left, right)]
    slice x1 -> x0, local copies, waits for them, and re-layouts: 0.98 us -> none  [body(): high = lax.ppermute(traces[:, :width], 'tm', [(b, a) for a, b in forward])]
    pallas_call x2 -> x4, Pallas kernels: 7.05 us -> 7.96 us  [the longest x1 3.5 us: shifted_rows(): pl.pallas_call(functools.partial(shifted_kernel, channels=channels), in_s...]
    sub x1 -> x0, other arithmetic: 0.68 us -> none  [body(): offset = source_index - owner * channels]
    eq x1 -> x0, other arithmetic: 0.67 us -> none  [body(): owner[None, :] == me]
    unnamed x6 -> x8, local copies, waits for them, and re-layouts: 2.19 us -> 2.42 us
  transfers between devices with their start and end apart: 7 -> 7, of which waited for: 1 -> 2; matrix products, arithmetic and copies ran while one was open for 5% -> 2% of each run, Pallas kernels for 12% -> 15%
where the time goes in v3:
time: 43.5 us; the launch traced here: 43.3 us
  Pallas kernels  25.1 us (58%)
  starting transfers between devices  10.1 us (23%)
  waiting for transfers between devices  3.76 us (9%)
  local copies, waits for them, and re-layouts  3.16 us (7%)
  other arithmetic  1.06 us (2%)
    pallas_call x1, Pallas kernels, correlate(): pl.pallas_call(functools.partial(correlate_kernel, sources=sources, chann...  17.2 us
    ppermute x5, starting transfers between devices, swap(): lax.ppermute(value, 'chan', [(i, i ^ distance) for i in range(owners)])  6.95 us
    ppermute x5, waiting for transfers between devices, swap(): lax.ppermute(value, 'chan', [(i, i ^ distance) for i in range(owners)])  3.75 us
    pallas_call x1, Pallas kernels, shifted_rows(): pl.pallas_call(functools.partial(shifted_kernel, channels=channels), in_s...  3.5 us
    ppermute x1, starting transfers between devices, body(): lax.ppermute(edge_b, 'tm', [(i, (i + 1 if i % 2 else i - 1) % slabs) for...  2.44 us
    unnamed x8, local copies, waits for them, and re-layouts  2.42 us
    pallas_call x1, Pallas kernels, normed_rows(): pl.pallas_call(functools.partial(normed_kernel, owners=owners, paired=pai...  2.27 us
    pallas_call x1, Pallas kernels, source_rows(): pl.pallas_call(source_kernel, in_specs=[SMEM] + [VMEM] * 6, out_specs=VME...  1.3 us
  transfers between devices with their start and end apart: 7, of which 2 were waited for; matrix products, arithmetic and copies ran while one was open for 2% of the time, Pallas kernels for 15%

profile of v3, /device:TPU:0, one launch (start us, length us, event | category | flops | bytes accessed | tf_op | source)
XLA Modules:
  0.0 43.3 jit_solution(16913099941783307883)
XLA Ops:
  0.0 1.0 %slice_select_fusion = (f32[80,384]{1,0:T(8,128)S(1)}, f32[80,384]{1,0:T(8,128)S(1)}) fusion(f32[80,2048]{1,0:T(8,128)} %traces.1, pred[]{:T(512)S(6)} %eq.6), kind=kLoop, calls=%fused_computation | loop fusion | flops 61440 | bytes 491521 | tf_op jit(solution)/shard_map/jit(_where)/select_n | solution.py:437
  1.0 2.4 %collective-permute-start.1 = (f32[80,384]{1,0:T(8,128)S(1)}, f32[80,384]{1,0:T(8,128)S(1)}, u32[]{:S(2)}, u32[]{:S(2)}) collective-permute-start(f32[80,384]{1,0:T(8,128)S(1)} %get-tuple-element.29), channel_id=1, source_target_pairs={{0,3},{1,2},{2,1},{3,0},{4,7},{5,6},{6,5},{7,4},{8,11},{9,10},{10,... | collective-permute-start | bytes 368648 | tf_op jit(solution)/shard_map/ppermute | solution.py:438
  3.4 0.7 %collective-permute-start = (f32[80,384]{1,0:T(8,128)S(1)}, f32[80,384]{1,0:T(8,128)S(1)}, u32[]{:S(2)}, u32[]{:S(2)}) collective-permute-start(f32[80,384]{1,0:T(8,128)S(1)} %get-tuple-element.30), channel_id=1, source_target_pairs={{0,1},{1,0},{2,3},{3,2},{4,5},{5,4},{6,7},{7,6},{8,9},{9,8},{10,11... | collective-permute-start | bytes 368648 | tf_op jit(solution)/shard_map/ppermute | solution.py:439
  4.1 0.7 %pad.4 = f32[384]{0:T(512)S(1)} pad(f32[65]{0:T(128)} %param.4, f32[]{:T(128)} %constant.26.clone.1), padding=96_223 | pad | bytes 1800 | tf_op jit(solution)/shard_map/jit(_pad)/pad | solution.py:433
  4.8 0.1 pad_add_fusion.place
  4.9 0.0 copy-start
  4.9 1.1 %copy-done = f32[80,2048]{1,0:T(8,128)S(1)} copy-done((f32[80,2048]{1,0:T(8,128)S(1)}, f32[80,2048]{1,0:T(8,128)}, u32[]{:S(2)}) %copy-start) | copy-done | bytes 655384
  6.0 0.0 copy-start.1
  6.0 0.7 %copy-done.1 = s32[64]{0:T(128)S(1)} copy-done((s32[64]{0:T(128)S(1)}, s32[64]{0:T(128)}, u32[]{:S(2)}) %copy-start.1) | copy-done | bytes 280
  6.7 0.9 %picked_rows.1 = (bf16[16,80]{1,0:T(8,128)(2,1)S(1)}, bf16[80,2048]{1,0:T(8,128)(2,1)S(1)}, bf16[80,2048]{1,0:T(8,128)(2,1)S(1)}, bf16[16,2048]{1,0:T(8,128)(2,1)S(1)}, bf16[16,2048]{1,0:T(8,128)(2,1)S(1)}) custom-call(s32[4]{0:T(128)S(1)} %pad_add_fusion.place, s32[1,64]{1,0:T(1,128)S(1)} %bitcast.7, f32[80,2048]{1,0:T(8,128)S(1)} %copy-done), custom_call_target="tpu_custom_call" | custom-call | tf_op jit(solution)/shard_map/picked_rows/pallas_call | solution.py:330
  7.6 0.0 collective-permute-done.1.got_b
  7.6 0.0 collective-permute-done.got_a
  7.6 1.3 %source_rows.1.refs_1_ = bf16[240,128]{1,0:T(8,128)(2,1)S(1)} custom-call(s32[4]{0:T(128)S(1)} %pad_add_fusion.place, bf16[16,80]{1,0:T(8,128)(2,1)S(1)} %get-tuple-element.20.pick, bf16[16,2048]{1,0:T(8,128)(2,1)S(1)} %get-tuple-element.21.rows_high, bf16[16,2048]{1,0:T(8,128)(2,1)S(1)} %get-tuple-element.22.rows_low, ...), custom_call_target="tpu_custom_call" | custom-call | tf_op jit(solution)/shard_map/source_rows/pallas_call | solution.py:342
  8.9 2.1 %collective-permute-start.5 = (bf16[240,128]{1,0:T(8,128)(2,1)S(1)}, bf16[240,128]{1,0:T(8,128)(2,1)S(1)}, u32[]{:S(2)}, u32[]{:S(2)}) collective-permute-start(bf16[240,128]{1,0:T(8,128)(2,1)S(1)} %source_rows.1.refs_1_), channel_id=1, source_target_pairs={{0,4},{4,0},{8,12},{12,8},{16,20},{20,16},{24,28},{28,24},{1,5},{5... | collective-permute-start | bytes 184328 | tf_op jit(solution)/shard_map/ppermute | solution.py:452
  11.0 3.6 %collective-permute-start.4 = (bf16[240,128]{1,0:T(8,128)(2,1)S(1)}, bf16[240,128]{1,0:T(8,128)(2,1)S(1)}, u32[]{:S(2)}, u32[]{:S(2)}) collective-permute-start(bf16[240,128]{1,0:T(8,128)(2,1)S(1)} %source_rows.1.refs_1_), channel_id=1, source_target_pairs={{0,24},{4,28},{8,16},{12,20},{16,8},{20,12},{24,0},{28,4},{1,25},{... | collective-permute-start | bytes 184328 | tf_op jit(solution)/shard_map/ppermute | solution.py:452
  14.6 0.0 collective-permute-start.3
  14.6 0.8 %collective-permute-start.2 = (bf16[240,128]{1,0:T(8,128)(2,1)S(1)}, bf16[240,128]{1,0:T(8,128)(2,1)S(1)}, u32[]{:S(2)}, u32[]{:S(2)}) collective-permute-start(bf16[240,128]{1,0:T(8,128)(2,1)S(1)} %source_rows.1.refs_1_), channel_id=1, source_target_pairs={{0,8},{4,12},{8,0},{12,4},{16,24},{20,28},{24,16},{28,20},{1,9},{5... | collective-permute-start | bytes 184328 | tf_op jit(solution)/shard_map/ppermute | solution.py:452
  15.3 0.0 copy-start.2
  15.4 0.7 %copy-done.2 = s32[64]{0:T(128)S(1)} copy-done((s32[64]{0:T(128)S(1)}, s32[64]{0:T(128)}, u32[]{:S(2)}) %copy-start.2) | copy-done | bytes 280
  16.0 2.3 %normed_rows.1 = (f32[1280,128]{1,0:T(8,128)S(1)}, s32[1,64]{1,0:T(1,128)S(1)}) custom-call(s32[4]{0:T(128)S(1)} %pad_add_fusion.place, s32[1,64]{1,0:T(1,128)S(1)} %bitcast.8, bf16[80,2048]{1,0:T(8,128)(2,1)S(1)} %get-tuple-element.17.high, bf16[80,2048]{1,0:T(8,128)(2,1)S(1)} %get-tuple-element.18.low, f32[80,384]{1,0:T(8,128)S(1)} %collective-permute-done.got_a, ...), custom_call_target="tpu_custom_call" | custom-call | flops 629145600 | bytes 2621440 | tf_op jit(solution)/shard_map/normed_rows/pallas_call | solution.py:354
  18.3 0.0 collective-permute-done.5.refs_3_
  18.3 0.0 collective-permute-done.4
  18.3 1.7 %collective-permute-done.3 = bf16[240,128]{1,0:T(8,128)(2,1)S(1)} collective-permute-done((bf16[240,128]{1,0:T(8,128)(2,1)S(1)}, bf16[240,128]{1,0:T(8,128)(2,1)S(1)}, u32[]{:S(2)}, u32[]{:S(2)}) %collective-permute-start.3) | collective-permute-done | bytes 61472 | tf_op jit(solution)/shard_map/ppermute | solution.py:452
  20.0 0.0 collective-permute-done.2
  20.0 0.5 %collective-permute-start.6 = (bf16[720,128]{1,0:T(8,128)(2,1)S(1)}, bf16[720,128]{1,0:T(8,128)(2,1)S(1)}, u32[]{:S(2)}, u32[]{:S(2)}) collective-permute-start(bf16[720,128]{1,0:T(8,128)(2,1)S(1)} %constant_dynamic-update-slice_fusion.refs_2_), channel_id=1, source_target_pairs={{0,4},{4,0},{8,12},{12,8},{16,20},{20,16},{24,28},{28,24},{1,5},{5... | collective-permute-start | bytes 552968 | tf_op jit(solution)/shard_map/ppermute | solution.py:452
  20.5 3.5 %shifted_rows.1.refs_5_ = bf16[2560,2304]{1,0:T(8,128)(2,1)S(1)} custom-call(f32[1280,128]{1,0:T(8,128)S(1)} %get-tuple-element.28.normed), custom_call_target="tpu_custom_call" | custom-call | flops 23592960 | bytes 11796480 | tf_op jit(solution)/shard_map/shifted_rows/pallas_call | solution.py:375
  24.0 2.1 %collective-permute-done.6.refs_4_ = bf16[720,128]{1,0:T(8,128)(2,1)S(1)} collective-permute-done((bf16[720,128]{1,0:T(8,128)(2,1)S(1)}, bf16[720,128]{1,0:T(8,128)(2,1)S(1)}, u32[]{:S(2)}, u32[]{:S(2)}) %collective-permute-start.6) | collective-permute-done | bytes 184352 | tf_op jit(solution)/shard_map/ppermute | solution.py:452
  26.1 17.2 %correlate.1 = f32[64,10,4,8,128]{4,3,2,1,0:T(8,128)} custom-call(s32[1,64]{1,0:T(1,128)S(1)} %get-tuple-element.19.refs_0_, bf16[240,128]{1,0:T(8,128)(2,1)S(1)} %source_rows.1.refs_1_, bf16[720,128]{1,0:T(8,128)(2,1)S(1)} %constant_dynamic-update-slice_fusion.refs_2_, bf16[240,128]{1,0:T(8,128)(2,1)S(1)} %collective-permute-done.5.refs_3_, ...), custom_call_target="tpu_custom_call" | custom-call | tf_op jit(solution)/shard_map/correlate/pallas_call | solution.py:394
  (4 shorter events, 0.0 us)
Async XLA Ops:
  1.0 6.6 %collective-permute-start.1 = (f32[80,384]{1,0:T(8,128)S(1)}, f32[80,384]{1,0:T(8,128)S(1)}, u32[]{:S(2)}, u32[]{:S(2)}) collective-permute-start(f32[80,384]{1,0:T(8,128)S(1)} %get-tuple-element.29), channel_id=1, source_target_pairs={{0,3},{1,2},{2,1},{3,0},{4,7},{5,6},{6,5},{7,4},{8,11},{9,10},{10,... | collective-permute-start | bytes 368648 | tf_op jit(solution)/shard_map/ppermute | solution.py:438
  3.4 4.1 %collective-permute-start = (f32[80,384]{1,0:T(8,128)S(1)}, f32[80,384]{1,0:T(8,128)S(1)}, u32[]{:S(2)}, u32[]{:S(2)}) collective-permute-start(f32[80,384]{1,0:T(8,128)S(1)} %get-tuple-element.30), channel_id=1, source_target_pairs={{0,1},{1,0},{2,3},{3,2},{4,5},{5,4},{6,7},{7,6},{8,9},{9,8},{10,11... | collective-permute-start | bytes 368648 | tf_op jit(solution)/shard_map/ppermute | solution.py:439
  4.9 1.1 %copy-start = (f32[80,2048]{1,0:T(8,128)S(1)}, f32[80,2048]{1,0:T(8,128)}, u32[]{:S(2)}) copy-start(f32[80,2048]{1,0:T(8,128)} %traces.1) | copy-start | bytes 1966084
  6.0 0.7 %copy-start.1 = (s32[64]{0:T(128)S(1)}, s32[64]{0:T(128)}, u32[]{:S(2)}) copy-start(s32[64]{0:T(128)} %param.5) | copy-start | bytes 772
  8.9 9.4 %collective-permute-start.5 = (bf16[240,128]{1,0:T(8,128)(2,1)S(1)}, bf16[240,128]{1,0:T(8,128)(2,1)S(1)}, u32[]{:S(2)}, u32[]{:S(2)}) collective-permute-start(bf16[240,128]{1,0:T(8,128)(2,1)S(1)} %source_rows.1.refs_1_), channel_id=1, source_target_pairs={{0,4},{4,0},{8,12},{12,8},{16,20},{20,16},{24,28},{28,24},{1,5},{5... | collective-permute-start | bytes 184328 | tf_op jit(solution)/shard_map/ppermute | solution.py:452
  11.0 7.3 %collective-permute-start.4 = (bf16[240,128]{1,0:T(8,128)(2,1)S(1)}, bf16[240,128]{1,0:T(8,128)(2,1)S(1)}, u32[]{:S(2)}, u32[]{:S(2)}) collective-permute-start(bf16[240,128]{1,0:T(8,128)(2,1)S(1)} %source_rows.1.refs_1_), channel_id=1, source_target_pairs={{0,24},{4,28},{8,16},{12,20},{16,8},{20,12},{24,0},{28,4},{1,25},{... | collective-permute-start | bytes 184328 | tf_op jit(solution)/shard_map/ppermute | solution.py:452
  14.6 5.4 %collective-permute-start.3 = (bf16[240,128]{1,0:T(8,128)(2,1)S(1)}, bf16[240,128]{1,0:T(8,128)(2,1)S(1)}, u32[]{:S(2)}, u32[]{:S(2)}) collective-permute-start(bf16[240,128]{1,0:T(8,128)(2,1)S(1)} %source_rows.1.refs_1_), channel_id=1, source_target_pairs={{0,16},{4,20},{8,24},{12,28},{16,0},{20,4},{24,8},{28,12},{1,17},{... | collective-permute-start | bytes 184328 | tf_op jit(solution)/shard_map/ppermute | solution.py:452
  14.6 5.4 %collective-permute-start.2 = (bf16[240,128]{1,0:T(8,128)(2,1)S(1)}, bf16[240,128]{1,0:T(8,128)(2,1)S(1)}, u32[]{:S(2)}, u32[]{:S(2)}) collective-permute-start(bf16[240,128]{1,0:T(8,128)(2,1)S(1)} %source_rows.1.refs_1_), channel_id=1, source_target_pairs={{0,8},{4,12},{8,0},{12,4},{16,24},{20,28},{24,16},{28,20},{1,9},{5... | collective-permute-start | bytes 184328 | tf_op jit(solution)/shard_map/ppermute | solution.py:452
  15.3 0.7 %copy-start.2 = (s32[64]{0:T(128)S(1)}, s32[64]{0:T(128)}, u32[]{:S(2)}) copy-start(s32[64]{0:T(128)} %param.5) | copy-start | bytes 772
  20.0 6.1 %collective-permute-start.6 = (bf16[720,128]{1,0:T(8,128)(2,1)S(1)}, bf16[720,128]{1,0:T(8,128)(2,1)S(1)}, u32[]{:S(2)}, u32[]{:S(2)}) collective-permute-start(bf16[720,128]{1,0:T(8,128)(2,1)S(1)} %constant_dynamic-update-slice_fusion.refs_2_), channel_id=1, source_target_pairs={{0,4},{4,0},{8,12},{12,8},{16,20},{20,16},{24,28},{28,24},{1,5},{5... | collective-permute-start | bytes 552968 | tf_op jit(solution)/shard_map/ppermute | solution.py:452

commit v4 on v3

--- a/solution.py
+++ b/solution.py
@@ -78,12 +78,13 @@
     return jnp.dot(left, right, preferred_element_type=F32)
 
 
-def pick_kernel(place, index, traces, pick, high, low, rows_high, rows_low):
+def pick_kernel(place, small, traces, pick, high, low, rows_high, rows_low):
     channels = traces.shape[0]
+    index = small[:, 3 * LANES :]
     sources = index.shape[1]
     channel = lax.broadcasted_iota(jnp.int32, (channels, sources), 0) + place[3] * channels
     number = lax.broadcasted_iota(jnp.int32, (channels, sources), 1).astype(F32)
-    equal = jnp.where(index[...] == channel, 1.0, 0.0)
+    equal = jnp.where(index == channel.astype(F32), 1.0, 0.0)
     here = jnp.sum(equal, axis=1, keepdims=True)
     order = jnp.sum(equal * number, axis=1, keepdims=True)
     across = lax.broadcasted_iota(jnp.int32, (ROWS, sources), 1).astype(F32).astype(BF16)
@@ -107,7 +108,7 @@
     return low, high
 
 
-def source_kernel(place, pick, rows_high, rows_low, got_a, got_b, taps_row, out):
+def source_kernel(place, pick, rows_high, rows_low, got_a, got_b, small, out):
     own = rows_high.shape[1] // LANES
 
     def blocks_of(high, low, count):
@@ -124,25 +125,26 @@
     pairs = [(nothing, nothing)] + sides[0] + blocks_of(rows_high, rows_low, own) + sides[1]
     pairs += [(nothing, nothing)]
     normed = normalize(
-        pairs, -SIDE - 1, own - 1, place[0] > 0, place[0] < place[1] - 1, taps_row[...]
+        pairs, -SIDE - 1, own - 1, place[0] > 0, place[0] < place[1] - 1, small[:, : 3 * LANES]
     )
     packed = jnp.concatenate([block[:MAX_OWN] for block in normed], axis=0)
     out[...] = packed.astype(BF16)
 
 
-def normed_kernel(place, index, high, low, got_a, got_b, taps_row, out, start, *, owners, paired):
+def normed_kernel(place, high, low, got_a, got_b, small, out, start, *, owners, paired):
     channels, samples = high.shape
     own = samples // LANES
+    index = small[:, 3 * LANES :]
     sources = index.shape[1]
-    line = jnp.broadcast_to(index[...], (sources, sources))
+    line = jnp.broadcast_to(index, (sources, sources))
     ahead = lax.broadcasted_iota(jnp.int32, (sources, sources), 0)
     behind = lax.broadcasted_iota(jnp.int32, (sources, sources), 1)
 
     def owner_of(value):
-        return ((value.astype(F32) + 0.5) * (1.0 / channels)).astype(jnp.int32)
-
-    upright = jnp.sum(jnp.where(ahead == behind, line, 0).astype(F32), axis=1, keepdims=True)
-    owner = owner_of(index[...])
+        return ((value + 0.5) * (1.0 / channels)).astype(jnp.int32)
+
+    upright = jnp.sum(jnp.where(ahead == behind, line, 0.0), axis=1, keepdims=True)
+    owner = owner_of(index)
     same = (owner_of(upright) == owner) & (ahead < behind)
     rank = jnp.sum(jnp.where(same, 1.0, 0.0), axis=0, keepdims=True).astype(jnp.int32)
     if paired:
@@ -158,7 +160,7 @@
         (high[:, b * LANES : (b + 1) * LANES], low[:, b * LANES : (b + 1) * LANES]) for b in range(own)
     ]
     pairs += [split(after[:, :LANES]), (nothing, nothing)]
-    normed = normalize(pairs, -2, own - 1, place[0] > 0, place[0] < place[1] - 1, taps_row[...])
+    normed = normalize(pairs, -2, own - 1, place[0] > 0, place[0] < place[1] - 1, small[:, : 3 * LANES])
     for b, block in enumerate(normed):
         out[b * channels : (b + 1) * channels, :] = block
 
@@ -219,6 +221,11 @@
             boxes.at[:, 0:UNITS, halves[0] : halves[-1] + 1],
             out.at[:, pl.ds(pair * UNITS, UNITS), halves[0] : halves[-1] + 1],
             sem.at[halves[0] // half_of],
+        )
+
+    def unit(m, q, which):
+        return pltpu.make_async_copy(
+            boxes.at[:, m, q], out.at[:, step * UNITS + m, q], sem.at[2 + which]
         )
 
     lane = lax.broadcasted_iota(jnp.int32, (sources, LANES), 1)
@@ -268,11 +275,12 @@
         for part in parts:
             all_rows[start : start + part.shape[0], :] = part[...].astype(F32)
             start += part.shape[0]
-        lines[blocks * sources :, :] = jnp.zeros((sources, LANES), F32)
+        pitch = sources + 8
+        lines[blocks * pitch : blocks * pitch + sources, :] = jnp.zeros((sources, LANES), F32)
         windows[:, samples + LANES :] = jnp.zeros((windows.shape[0], depth - samples - LANES), BF16)
 
         for s in range(sources):
-            lines[pl.ds(s, blocks, stride=sources), :] = all_rows[
+            lines[pl.ds(s, blocks, stride=pitch), :] = all_rows[
                 pl.ds(place[0, s], blocks, stride=MAX_OWN), :
             ]
 
@@ -280,7 +288,7 @@
             turn = p * LAG_WIDTH
             turned = None
             for b in range(blocks + 1):
-                line = lines[b * sources : (b + 1) * sources, :]
+                line = lines[b * pitch : b * pitch + sources, :]
                 following = pltpu.roll(line, LANES - turn, 1) if p else line
                 if b:
                     block = b - 1
@@ -311,19 +319,20 @@
         def _():
             send(step - 1, second).wait()
 
-        for q in second:
-            for m in range(UNITS):
-                arrange(m, q)
-        send(step, second).start()
+        left = [(m, q) for q in second for m in range(UNITS)]
+        for i, (m, q) in enumerate(left):
+            arrange(m, q)
+            unit(m, q, i).start()
         send(step, first).wait()
-        send(step, second).wait()
+        for i, (m, q) in enumerate(left):
+            unit(m, q, i).wait()
 
 
 SMEM = pl.BlockSpec(memory_space=pltpu.SMEM)
 VMEM = pl.BlockSpec(memory_space=pltpu.VMEM)
 
 
-def picked_rows(place, index, traces):
+def picked_rows(place, small, traces):
     channels, samples = traces.shape
     slab = jax.ShapeDtypeStruct(traces.shape, BF16)
     rows = jax.ShapeDtypeStruct((ROWS, samples), BF16)
@@ -334,10 +343,10 @@
         out_shape=[jax.ShapeDtypeStruct((ROWS, channels), BF16), slab, slab, rows, rows],
         compiler_params=pltpu.CompilerParams(vmem_limit_bytes=8 * MIB),
         name="picked_rows",
-    )(place, index[None], traces)
-
-
-def source_rows(place, pick, rows_high, rows_low, got_a, got_b, taps_row):
+    )(place, small, traces)
+
+
+def source_rows(place, pick, rows_high, rows_low, got_a, got_b, small):
     blocks = rows_high.shape[1] // LANES + 2 * EDGE
     return pl.pallas_call(
         source_kernel,
@@ -346,18 +355,18 @@
         out_shape=jax.ShapeDtypeStruct((blocks * MAX_OWN, LANES), BF16),
         compiler_params=pltpu.CompilerParams(vmem_limit_bytes=8 * MIB),
         name="source_rows",
-    )(place, pick, rows_high, rows_low, got_a, got_b, taps_row)
-
-
-def normed_rows(place, index, high, low, got_a, got_b, taps_row, owners, paired):
+    )(place, pick, rows_high, rows_low, got_a, got_b, small)
+
+
+def normed_rows(place, small, high, low, got_a, got_b, owners, paired):
     channels, samples = high.shape
     return pl.pallas_call(
         functools.partial(normed_kernel, owners=owners, paired=paired),
-        in_specs=[SMEM] + [VMEM] * 6,
+        in_specs=[SMEM] + [VMEM] * 5,
         out_specs=[VMEM] * 2,
         out_shape=[
             jax.ShapeDtypeStruct((channels * samples // LANES, LANES), F32),
-            jax.ShapeDtypeStruct((1, index.shape[0]), jnp.int32),
+            jax.ShapeDtypeStruct((1, small.shape[1] - 3 * LANES), jnp.int32),
         ],
         compiler_params=pltpu.CompilerParams(vmem_limit_bytes=24 * MIB),
         cost_estimate=pl.CostEstimate(
@@ -366,7 +375,7 @@
             transcendentals=0,
         ),
         name="normed_rows",
-    )(place, index[None], high, low, got_a, got_b, taps_row)
+    )(place, high, low, got_a, got_b, small)
 
 
 def shifted_rows(normed, channels):
@@ -408,10 +417,10 @@
         ),
         scratch_shapes=[
             pltpu.VMEM((rows, LANES), F32),
-            pltpu.VMEM(((blocks + 1) * sources, LANES), F32),
+            pltpu.VMEM(((blocks + 1) * (sources + 8), LANES), F32),
             pltpu.VMEM((LAG_BLOCKS * PIECES * sources, shifted.shape[1]), BF16),
             pltpu.VMEM((sources * (UNITS + 1) * (LAG_BLOCKS + 1) * GROUP, LANES), F32),
-            pltpu.SemaphoreType.DMA((2,)),
+            pltpu.SemaphoreType.DMA((2 + UNITS * LAG_BLOCKS // 2,)),
         ],
         compiler_params=pltpu.CompilerParams(vmem_limit_bytes=24 * MIB),
         name="correlate",
@@ -430,7 +439,9 @@
     place = jnp.stack([slab, jnp.full_like(slab, slabs), parity, lax.axis_index("chan")])
     place = place.astype(jnp.int32)
     lead = LANES - (taps - 1) // 2
-    taps_row = jnp.pad(fir_taps, (lead, 3 * LANES - lead - taps))[None]
+    total = 3 * LANES + source_index.shape[0]
+    small = jnp.pad(fir_taps[None], ((0, 0), (lead, total - lead - taps)))
+    small = small + jnp.pad(source_index[None].astype(F32), ((0, 0), (3 * LANES, 0)))
 
     left, right = traces[:, : SIDE * LANES], traces[:, samples - SIDE * LANES :]
     if in_pairs:
@@ -440,12 +451,10 @@
     else:
         got_b = lax.ppermute(right, "tm", [(i, i + 1) for i in range(slabs - 1)])
         got_a = lax.ppermute(left, "tm", [(i + 1, i) for i in range(slabs - 1)])
-    pick, high, low, *rows = picked_rows(place, source_index, traces)
-    own = source_rows(place, pick, *rows, got_a, got_b, taps_row)
+    pick, high, low, *rows = picked_rows(place, small, traces)
+    own = source_rows(place, pick, *rows, got_a, got_b, small)
     paired = owners in (4, 8)
-    normed, start = normed_rows(
-        place, source_index, high, low, got_a, got_b, taps_row, owners, paired
-    )
+    normed, start = normed_rows(place, small, high, low, got_a, got_b, owners, paired)
     if paired:
 
         def swap(value, distance):

time: 43.5 us -> 43 us (0.989)
  local copies, waits for them, and re-layouts: 3.16 us -> 1.12 us
  other arithmetic: 1.06 us -> 2.44 us
  waiting for transfers between devices: 3.76 us -> 4.41 us
    unnamed x8 -> x4, local copies, waits for them, and re-layouts: 2.42 us -> 1.11 us
    add x0 -> x1, other arithmetic: none -> 0.73 us  [body(): small + jnp.pad(source_index[None].astype(F32), ((0, 0), (3 * LANES, 0)))]
    pad x1 -> x0, local copies, waits for them, and re-layouts: 0.73 us -> none  [body(): taps_row = jnp.pad(fir_taps, (lead, 3 * LANES - lead - taps))[None]]
    convert_element_type x0 -> x1, other arithmetic: none -> 0.66 us  [body(): source_index[None].astype(F32)]
    ppermute x5, waiting for transfers between devices: 3.75 us -> 4.41 us  [swap(): lax.ppermute(value, 'chan', [(i, i ^ distance) for i in range(owners)])]
    pallas_call x1, Pallas kernels: 17.2 us -> 16.7 us  [correlate(): pl.pallas_call(functools.partial(correlate_kernel, sources=sources, chann...]
  transfers between devices with their start and end apart: 7 -> 7, of which waited for: 2 -> 2; matrix products, arithmetic and copies ran while one was open for 2% -> 3% of each run, Pallas kernels for 15% -> 16%
where the time goes in v4:
time: 43 us; the launch traced here: 42.8 us
  Pallas kernels  24.7 us (57%)
  starting transfers between devices  10.1 us (23%)
  waiting for transfers between devices  4.41 us (10%)
  other arithmetic  2.44 us (6%)
  local copies, waits for them, and re-layouts  1.12 us (3%)
    pallas_call x1, Pallas kernels, correlate(): pl.pallas_call(functools.partial(correlate_kernel, sources=sources, chann...  16.7 us
    ppermute x5, starting transfers between devices, swap(): lax.ppermute(value, 'chan', [(i, i ^ distance) for i in range(owners)])  6.95 us
    ppermute x5, waiting for transfers between devices, swap(): lax.ppermute(value, 'chan', [(i, i ^ distance) for i in range(owners)])  4.41 us
    pallas_call x1, Pallas kernels, shifted_rows(): pl.pallas_call(functools.partial(shifted_kernel, channels=channels), in_s...  3.5 us
    ppermute x1, starting transfers between devices, body(): lax.ppermute(edge_b, 'tm', [(i, (i + 1 if i % 2 else i - 1) % slabs) for...  2.44 us
    pallas_call x1, Pallas kernels, normed_rows(): pl.pallas_call(functools.partial(normed_kernel, owners=owners, paired=pai...  2.27 us
    pallas_call x1, Pallas kernels, source_rows(): pl.pallas_call(source_kernel, in_specs=[SMEM] + [VMEM] * 6, out_specs=VME...  1.3 us
    unnamed x4, local copies, waits for them, and re-layouts  1.11 us
  transfers between devices with their start and end apart: 7, of which 2 were waited for; matrix products, arithmetic and copies ran while one was open for 3% of the time, Pallas kernels for 16%

profile of v4, /device:TPU:0, one launch (start us, length us, event | category | flops | bytes accessed | tf_op | source)
XLA Modules:
  0.0 42.8 jit_solution(14927271107315412647)
XLA Ops:
  0.0 1.0 %slice_select_fusion = (f32[80,384]{1,0:T(8,128)S(1)}, f32[80,384]{1,0:T(8,128)S(1)}) fusion(f32[80,2048]{1,0:T(8,128)} %traces.1, pred[]{:T(512)S(6)} %eq.6), kind=kLoop, calls=%fused_computation | loop fusion | flops 61440 | bytes 491521 | tf_op jit(solution)/shard_map/jit(_where)/select_n | solution.py:448
  1.0 2.4 %collective-permute-start.1 = (f32[80,384]{1,0:T(8,128)S(1)}, f32[80,384]{1,0:T(8,128)S(1)}, u32[]{:S(2)}, u32[]{:S(2)}) collective-permute-start(f32[80,384]{1,0:T(8,128)S(1)} %get-tuple-element.29), channel_id=1, source_target_pairs={{0,3},{1,2},{2,1},{3,0},{4,7},{5,6},{6,5},{7,4},{8,11},{9,10},{10,... | collective-permute-start | bytes 368648 | tf_op jit(solution)/shard_map/ppermute | solution.py:449
  3.4 0.7 %collective-permute-start = (f32[80,384]{1,0:T(8,128)S(1)}, f32[80,384]{1,0:T(8,128)S(1)}, u32[]{:S(2)}, u32[]{:S(2)}) collective-permute-start(f32[80,384]{1,0:T(8,128)S(1)} %get-tuple-element.30), channel_id=1, source_target_pairs={{0,1},{1,0},{2,3},{3,2},{4,5},{5,4},{6,7},{7,6},{8,9},{9,8},{10,11... | collective-permute-start | bytes 368648 | tf_op jit(solution)/shard_map/ppermute | solution.py:450
  4.1 0.7 %convert_bitcast_fusion = f32[1,64]{1,0:T(1,128)S(1)} fusion(s32[64]{0:T(128)} %param.5), kind=kLoop, calls=%fused_computation.7 | loop fusion | flops 64 | bytes 512 | tf_op jit(solution)/shard_map/convert_element_type | solution.py:444
  4.8 0.1 pad_add_fusion.1.place
  4.8 0.7 %pad_add_fusion.small = f32[1,448]{1,0:T(1,128)S(1)} fusion(f32[1,64]{1,0:T(1,128)S(1)} %convert_bitcast_fusion, f32[1,65]{1,0:T(1,128)} %bitcast.9), kind=kLoop, calls=%fused_computation.5 | loop fusion | flops 448 | bytes 2308 | tf_op jit(solution)/shard_map/add | solution.py:444
  5.6 0.0 copy-start
  5.6 1.1 %copy-done = f32[80,2048]{1,0:T(8,128)S(1)} copy-done((f32[80,2048]{1,0:T(8,128)S(1)}, f32[80,2048]{1,0:T(8,128)}, u32[]{:S(2)}) %copy-start) | copy-done | bytes 655384
  6.7 0.9 %picked_rows.1 = (bf16[16,80]{1,0:T(8,128)(2,1)S(1)}, bf16[80,2048]{1,0:T(8,128)(2,1)S(1)}, bf16[80,2048]{1,0:T(8,128)(2,1)S(1)}, bf16[16,2048]{1,0:T(8,128)(2,1)S(1)}, bf16[16,2048]{1,0:T(8,128)(2,1)S(1)}) custom-call(s32[4]{0:T(128)S(1)} %pad_add_fusion.1.place, f32[1,448]{1,0:T(1,128)S(1)} %pad_add_fusion.small, f32[80,2048]{1,0:T(8,128)S(1)} %copy-done), custom_call_target="tpu_custom_call" | custom-call | tf_op jit(solution)/shard_map/picked_rows/pallas_call | solution.py:339
  7.6 0.0 collective-permute-done.1.got_b
  7.6 0.0 collective-permute-done.got_a
  7.6 1.3 %source_rows.1.refs_1_ = bf16[240,128]{1,0:T(8,128)(2,1)S(1)} custom-call(s32[4]{0:T(128)S(1)} %pad_add_fusion.1.place, bf16[16,80]{1,0:T(8,128)(2,1)S(1)} %get-tuple-element.20.pick, bf16[16,2048]{1,0:T(8,128)(2,1)S(1)} %get-tuple-element.21.rows_high, bf16[16,2048]{1,0:T(8,128)(2,1)S(1)} %get-tuple-element.22.rows_low, ...), custom_call_target="tpu_custom_call" | custom-call | tf_op jit(solution)/shard_map/source_rows/pallas_call | solution.py:351
  8.9 2.1 %collective-permute-start.5 = (bf16[240,128]{1,0:T(8,128)(2,1)S(1)}, bf16[240,128]{1,0:T(8,128)(2,1)S(1)}, u32[]{:S(2)}, u32[]{:S(2)}) collective-permute-start(bf16[240,128]{1,0:T(8,128)(2,1)S(1)} %source_rows.1.refs_1_), channel_id=1, source_target_pairs={{0,4},{4,0},{8,12},{12,8},{16,20},{20,16},{24,28},{28,24},{1,5},{5... | collective-permute-start | bytes 184328 | tf_op jit(solution)/shard_map/ppermute | solution.py:461
  11.0 3.6 %collective-permute-start.4 = (bf16[240,128]{1,0:T(8,128)(2,1)S(1)}, bf16[240,128]{1,0:T(8,128)(2,1)S(1)}, u32[]{:S(2)}, u32[]{:S(2)}) collective-permute-start(bf16[240,128]{1,0:T(8,128)(2,1)S(1)} %source_rows.1.refs_1_), channel_id=1, source_target_pairs={{0,24},{4,28},{8,16},{12,20},{16,8},{20,12},{24,0},{28,4},{1,25},{... | collective-permute-start | bytes 184328 | tf_op jit(solution)/shard_map/ppermute | solution.py:461
  14.6 0.0 collective-permute-start.3
  14.6 0.8 %collective-permute-start.2 = (bf16[240,128]{1,0:T(8,128)(2,1)S(1)}, bf16[240,128]{1,0:T(8,128)(2,1)S(1)}, u32[]{:S(2)}, u32[]{:S(2)}) collective-permute-start(bf16[240,128]{1,0:T(8,128)(2,1)S(1)} %source_rows.1.refs_1_), channel_id=1, source_target_pairs={{0,8},{4,12},{8,0},{12,4},{16,24},{20,28},{24,16},{28,20},{1,9},{5... | collective-permute-start | bytes 184328 | tf_op jit(solution)/shard_map/ppermute | solution.py:461
  15.3 2.3 %normed_rows.1 = (f32[1280,128]{1,0:T(8,128)S(1)}, s32[1,64]{1,0:T(1,128)S(1)}) custom-call(s32[4]{0:T(128)S(1)} %pad_add_fusion.1.place, bf16[80,2048]{1,0:T(8,128)(2,1)S(1)} %get-tuple-element.17.high, bf16[80,2048]{1,0:T(8,128)(2,1)S(1)} %get-tuple-element.18.low, f32[80,384]{1,0:T(8,128)S(1)} %collective-permute-done.got_a, ...), custom_call_target="tpu_custom_call" | custom-call | flops 629145600 | bytes 2621440 | tf_op jit(solution)/shard_map/normed_rows/pallas_call | solution.py:363
  17.6 0.0 collective-permute-done.5.refs_3_
  17.6 0.0 collective-permute-done.4
  17.6 2.3 %collective-permute-done.3 = bf16[240,128]{1,0:T(8,128)(2,1)S(1)} collective-permute-done((bf16[240,128]{1,0:T(8,128)(2,1)S(1)}, bf16[240,128]{1,0:T(8,128)(2,1)S(1)}, u32[]{:S(2)}, u32[]{:S(2)}) %collective-permute-start.3) | collective-permute-done | bytes 61472 | tf_op jit(solution)/shard_map/ppermute | solution.py:461
  20.0 0.0 collective-permute-done.2
  20.0 0.5 %collective-permute-start.6 = (bf16[720,128]{1,0:T(8,128)(2,1)S(1)}, bf16[720,128]{1,0:T(8,128)(2,1)S(1)}, u32[]{:S(2)}, u32[]{:S(2)}) collective-permute-start(bf16[720,128]{1,0:T(8,128)(2,1)S(1)} %constant_dynamic-update-slice_fusion.refs_2_), channel_id=1, source_target_pairs={{0,4},{4,0},{8,12},{12,8},{16,20},{20,16},{24,28},{28,24},{1,5},{5... | collective-permute-start | bytes 552968 | tf_op jit(solution)/shard_map/ppermute | solution.py:461
  20.5 3.5 %shifted_rows.1.refs_5_ = bf16[2560,2304]{1,0:T(8,128)(2,1)S(1)} custom-call(f32[1280,128]{1,0:T(8,128)S(1)} %get-tuple-element.28.normed), custom_call_target="tpu_custom_call" | custom-call | flops 23592960 | bytes 11796480 | tf_op jit(solution)/shard_map/shifted_rows/pallas_call | solution.py:384
  24.0 2.1 %collective-permute-done.6.refs_4_ = bf16[720,128]{1,0:T(8,128)(2,1)S(1)} collective-permute-done((bf16[720,128]{1,0:T(8,128)(2,1)S(1)}, bf16[720,128]{1,0:T(8,128)(2,1)S(1)}, u32[]{:S(2)}, u32[]{:S(2)}) %collective-permute-start.6) | collective-permute-done | bytes 184352 | tf_op jit(solution)/shard_map/ppermute | solution.py:461
  26.1 16.7 %correlate.1 = f32[64,10,4,8,128]{4,3,2,1,0:T(8,128)} custom-call(s32[1,64]{1,0:T(1,128)S(1)} %get-tuple-element.19.refs_0_, bf16[240,128]{1,0:T(8,128)(2,1)S(1)} %source_rows.1.refs_1_, bf16[720,128]{1,0:T(8,128)(2,1)S(1)} %constant_dynamic-update-slice_fusion.refs_2_, bf16[240,128]{1,0:T(8,128)(2,1)S(1)} %collective-permute-done.5.refs_3_, ...), custom_call_target="tpu_custom_call" | custom-call | tf_op jit(solution)/shard_map/correlate/pallas_call | solution.py:403
  (3 shorter events, 0.0 us)
Async XLA Ops:
  1.0 6.6 %collective-permute-start.1 = (f32[80,384]{1,0:T(8,128)S(1)}, f32[80,384]{1,0:T(8,128)S(1)}, u32[]{:S(2)}, u32[]{:S(2)}) collective-permute-start(f32[80,384]{1,0:T(8,128)S(1)} %get-tuple-element.29), channel_id=1, source_target_pairs={{0,3},{1,2},{2,1},{3,0},{4,7},{5,6},{6,5},{7,4},{8,11},{9,10},{10,... | collective-permute-start | bytes 368648 | tf_op jit(solution)/shard_map/ppermute | solution.py:449
  3.4 4.1 %collective-permute-start = (f32[80,384]{1,0:T(8,128)S(1)}, f32[80,384]{1,0:T(8,128)S(1)}, u32[]{:S(2)}, u32[]{:S(2)}) collective-permute-start(f32[80,384]{1,0:T(8,128)S(1)} %get-tuple-element.30), channel_id=1, source_target_pairs={{0,1},{1,0},{2,3},{3,2},{4,5},{5,4},{6,7},{7,6},{8,9},{9,8},{10,11... | collective-permute-start | bytes 368648 | tf_op jit(solution)/shard_map/ppermute | solution.py:450
  5.6 1.1 %copy-start = (f32[80,2048]{1,0:T(8,128)S(1)}, f32[80,2048]{1,0:T(8,128)}, u32[]{:S(2)}) copy-start(f32[80,2048]{1,0:T(8,128)} %traces.1) | copy-start | bytes 1966084
  8.9 8.8 %collective-permute-start.5 = (bf16[240,128]{1,0:T(8,128)(2,1)S(1)}, bf16[240,128]{1,0:T(8,128)(2,1)S(1)}, u32[]{:S(2)}, u32[]{:S(2)}) collective-permute-start(bf16[240,128]{1,0:T(8,128)(2,1)S(1)} %source_rows.1.refs_1_), channel_id=1, source_target_pairs={{0,4},{4,0},{8,12},{12,8},{16,20},{20,16},{24,28},{28,24},{1,5},{5... | collective-permute-start | bytes 184328 | tf_op jit(solution)/shard_map/ppermute | solution.py:461
  11.0 6.7 %collective-permute-start.4 = (bf16[240,128]{1,0:T(8,128)(2,1)S(1)}, bf16[240,128]{1,0:T(8,128)(2,1)S(1)}, u32[]{:S(2)}, u32[]{:S(2)}) collective-permute-start(bf16[240,128]{1,0:T(8,128)(2,1)S(1)} %source_rows.1.refs_1_), channel_id=1, source_target_pairs={{0,24},{4,28},{8,16},{12,20},{16,8},{20,12},{24,0},{28,4},{1,25},{... | collective-permute-start | bytes 184328 | tf_op jit(solution)/shard_map/ppermute | solution.py:461
  14.6 5.4 %collective-permute-start.3 = (bf16[240,128]{1,0:T(8,128)(2,1)S(1)}, bf16[240,128]{1,0:T(8,128)(2,1)S(1)}, u32[]{:S(2)}, u32[]{:S(2)}) collective-permute-start(bf16[240,128]{1,0:T(8,128)(2,1)S(1)} %source_rows.1.refs_1_), channel_id=1, source_target_pairs={{0,16},{4,20},{8,24},{12,28},{16,0},{20,4},{24,8},{28,12},{1,17},{... | collective-permute-start | bytes 184328 | tf_op jit(solution)/shard_map/ppermute | solution.py:461
  14.6 5.4 %collective-permute-start.2 = (bf16[240,128]{1,0:T(8,128)(2,1)S(1)}, bf16[240,128]{1,0:T(8,128)(2,1)S(1)}, u32[]{:S(2)}, u32[]{:S(2)}) collective-permute-start(bf16[240,128]{1,0:T(8,128)(2,1)S(1)} %source_rows.1.refs_1_), channel_id=1, source_target_pairs={{0,8},{4,12},{8,0},{12,4},{16,24},{20,28},{24,16},{28,20},{1,9},{5... | collective-permute-start | bytes 184328 | tf_op jit(solution)/shard_map/ppermute | solution.py:461
  20.0 6.1 %collective-permute-start.6 = (bf16[720,128]{1,0:T(8,128)(2,1)S(1)}, bf16[720,128]{1,0:T(8,128)(2,1)S(1)}, u32[]{:S(2)}, u32[]{:S(2)}) collective-permute-start(bf16[720,128]{1,0:T(8,128)(2,1)S(1)} %constant_dynamic-update-slice_fusion.refs_2_), channel_id=1, source_target_pairs={{0,4},{4,0},{8,12},{12,8},{16,20},{20,16},{24,28},{28,24},{1,5},{5... | collective-permute-start | bytes 552968 | tf_op jit(solution)/shard_map/ppermute | solution.py:461

commit v5 on v4

--- a/solution.py
+++ b/solution.py
@@ -399,6 +399,7 @@
 def correlate(place, parts, shifted, sources, channels, samples):
     blocks = samples // LANES + 2 * EDGE
     rows = sum(part.shape[0] for part in parts)
+    spare = -blocks % 8
     scale = 1.0 / math.sqrt(samples)
     boxes = pl.pallas_call(
         functools.partial(
@@ -416,8 +417,8 @@
             (sources, channels // GROUP, LAG_BLOCKS, GROUP, LANES), F32
         ),
         scratch_shapes=[
-            pltpu.VMEM((rows, LANES), F32),
-            pltpu.VMEM(((blocks + 1) * (sources + 8), LANES), F32),
+            pltpu.VMEM((rows + spare * MAX_OWN, LANES), F32),
+            pltpu.VMEM(((blocks + 1 + spare) * (sources + 8), LANES), F32),
             pltpu.VMEM((LAG_BLOCKS * PIECES * sources, shifted.shape[1]), BF16),
             pltpu.VMEM((sources * (UNITS + 1) * (LAG_BLOCKS + 1) * GROUP, LANES), F32),
             pltpu.SemaphoreType.DMA((2 + UNITS * LAG_BLOCKS // 2,)),

time: 43 us -> 43 us (level)
  no operation moved by 1% of the time
where the time goes in v5:
time: 43 us; the launch traced here: 42.8 us
  Pallas kernels  24.7 us (57%)
  starting transfers between devices  10.1 us (23%)
  waiting for transfers between devices  4.41 us (10%)
  other arithmetic  2.44 us (6%)
  local copies, waits for them, and re-layouts  1.12 us (3%)
    pallas_call x1, Pallas kernels, correlate(): pl.pallas_call(functools.partial(correlate_kernel, sources=sources, chann...  16.7 us
    ppermute x5, starting transfers between devices, swap(): lax.ppermute(value, 'chan', [(i, i ^ distance) for i in range(owners)])  6.95 us
    ppermute x5, waiting for transfers between devices, swap(): lax.ppermute(value, 'chan', [(i, i ^ distance) for i in range(owners)])  4.41 us
    pallas_call x1, Pallas kernels, shifted_rows(): pl.pallas_call(functools.partial(shifted_kernel, channels=channels), in_s...  3.5 us
    ppermute x1, starting transfers between devices, body(): lax.ppermute(edge_b, 'tm', [(i, (i + 1 if i % 2 else i - 1) % slabs) for...  2.44 us
    pallas_call x1, Pallas kernels, normed_rows(): pl.pallas_call(functools.partial(normed_kernel, owners=owners, paired=pai...  2.27 us
    pallas_call x1, Pallas kernels, source_rows(): pl.pallas_call(source_kernel, in_specs=[SMEM] + [VMEM] * 6, out_specs=VME...  1.3 us
    unnamed x4, local copies, waits for them, and re-layouts  1.11 us
  transfers between devices with their start and end apart: 7, of which 2 were waited for; matrix products, arithmetic and copies ran while one was open for 3% of the time, Pallas kernels for 16%

profile of v5, /device:TPU:0, one launch (start us, length us, event | category | flops | bytes accessed | tf_op | source)
XLA Modules:
  0.0 42.8 jit_solution(1264608340370330115)
XLA Ops:
  0.0 1.0 %slice_select_fusion = (f32[80,384]{1,0:T(8,128)S(1)}, f32[80,384]{1,0:T(8,128)S(1)}) fusion(f32[80,2048]{1,0:T(8,128)} %traces.1, pred[]{:T(512)S(6)} %eq.6), kind=kLoop, calls=%fused_computation | loop fusion | flops 61440 | bytes 491521 | tf_op jit(solution)/shard_map/jit(_where)/select_n | solution.py:449
  1.0 2.4 %collective-permute-start.1 = (f32[80,384]{1,0:T(8,128)S(1)}, f32[80,384]{1,0:T(8,128)S(1)}, u32[]{:S(2)}, u32[]{:S(2)}) collective-permute-start(f32[80,384]{1,0:T(8,128)S(1)} %get-tuple-element.29), channel_id=1, source_target_pairs={{0,3},{1,2},{2,1},{3,0},{4,7},{5,6},{6,5},{7,4},{8,11},{9,10},{10,... | collective-permute-start | bytes 368648 | tf_op jit(solution)/shard_map/ppermute | solution.py:450
  3.4 0.7 %collective-permute-start = (f32[80,384]{1,0:T(8,128)S(1)}, f32[80,384]{1,0:T(8,128)S(1)}, u32[]{:S(2)}, u32[]{:S(2)}) collective-permute-start(f32[80,384]{1,0:T(8,128)S(1)} %get-tuple-element.30), channel_id=1, source_target_pairs={{0,1},{1,0},{2,3},{3,2},{4,5},{5,4},{6,7},{7,6},{8,9},{9,8},{10,11... | collective-permute-start | bytes 368648 | tf_op jit(solution)/shard_map/ppermute | solution.py:451
  4.1 0.7 %convert_bitcast_fusion = f32[1,64]{1,0:T(1,128)S(1)} fusion(s32[64]{0:T(128)} %param.5), kind=kLoop, calls=%fused_computation.7 | loop fusion | flops 64 | bytes 512 | tf_op jit(solution)/shard_map/convert_element_type | solution.py:445
  4.8 0.1 pad_add_fusion.1.place
  4.8 0.7 %pad_add_fusion.small = f32[1,448]{1,0:T(1,128)S(1)} fusion(f32[1,64]{1,0:T(1,128)S(1)} %convert_bitcast_fusion, f32[1,65]{1,0:T(1,128)} %bitcast.9), kind=kLoop, calls=%fused_computation.5 | loop fusion | flops 448 | bytes 2308 | tf_op jit(solution)/shard_map/add | solution.py:445
  5.6 0.0 copy-start
  5.6 1.1 %copy-done = f32[80,2048]{1,0:T(8,128)S(1)} copy-done((f32[80,2048]{1,0:T(8,128)S(1)}, f32[80,2048]{1,0:T(8,128)}, u32[]{:S(2)}) %copy-start) | copy-done | bytes 655384
  6.7 0.9 %picked_rows.1 = (bf16[16,80]{1,0:T(8,128)(2,1)S(1)}, bf16[80,2048]{1,0:T(8,128)(2,1)S(1)}, bf16[80,2048]{1,0:T(8,128)(2,1)S(1)}, bf16[16,2048]{1,0:T(8,128)(2,1)S(1)}, bf16[16,2048]{1,0:T(8,128)(2,1)S(1)}) custom-call(s32[4]{0:T(128)S(1)} %pad_add_fusion.1.place, f32[1,448]{1,0:T(1,128)S(1)} %pad_add_fusion.small, f32[80,2048]{1,0:T(8,128)S(1)} %copy-done), custom_call_target="tpu_custom_call" | custom-call | tf_op jit(solution)/shard_map/picked_rows/pallas_call | solution.py:339
  7.6 0.0 collective-permute-done.1.got_b
  7.6 0.0 collective-permute-done.got_a
  7.6 1.3 %source_rows.1.refs_1_ = bf16[240,128]{1,0:T(8,128)(2,1)S(1)} custom-call(s32[4]{0:T(128)S(1)} %pad_add_fusion.1.place, bf16[16,80]{1,0:T(8,128)(2,1)S(1)} %get-tuple-element.20.pick, bf16[16,2048]{1,0:T(8,128)(2,1)S(1)} %get-tuple-element.21.rows_high, bf16[16,2048]{1,0:T(8,128)(2,1)S(1)} %get-tuple-element.22.rows_low, ...), custom_call_target="tpu_custom_call" | custom-call | tf_op jit(solution)/shard_map/source_rows/pallas_call | solution.py:351
  8.9 2.1 %collective-permute-start.5 = (bf16[240,128]{1,0:T(8,128)(2,1)S(1)}, bf16[240,128]{1,0:T(8,128)(2,1)S(1)}, u32[]{:S(2)}, u32[]{:S(2)}) collective-permute-start(bf16[240,128]{1,0:T(8,128)(2,1)S(1)} %source_rows.1.refs_1_), channel_id=1, source_target_pairs={{0,4},{4,0},{8,12},{12,8},{16,20},{20,16},{24,28},{28,24},{1,5},{5... | collective-permute-start | bytes 184328 | tf_op jit(solution)/shard_map/ppermute | solution.py:462
  11.0 3.6 %collective-permute-start.4 = (bf16[240,128]{1,0:T(8,128)(2,1)S(1)}, bf16[240,128]{1,0:T(8,128)(2,1)S(1)}, u32[]{:S(2)}, u32[]{:S(2)}) collective-permute-start(bf16[240,128]{1,0:T(8,128)(2,1)S(1)} %source_rows.1.refs_1_), channel_id=1, source_target_pairs={{0,24},{4,28},{8,16},{12,20},{16,8},{20,12},{24,0},{28,4},{1,25},{... | collective-permute-start | bytes 184328 | tf_op jit(solution)/shard_map/ppermute | solution.py:462
  14.6 0.0 collective-permute-start.3
  14.6 0.8 %collective-permute-start.2 = (bf16[240,128]{1,0:T(8,128)(2,1)S(1)}, bf16[240,128]{1,0:T(8,128)(2,1)S(1)}, u32[]{:S(2)}, u32[]{:S(2)}) collective-permute-start(bf16[240,128]{1,0:T(8,128)(2,1)S(1)} %source_rows.1.refs_1_), channel_id=1, source_target_pairs={{0,8},{4,12},{8,0},{12,4},{16,24},{20,28},{24,16},{28,20},{1,9},{5... | collective-permute-start | bytes 184328 | tf_op jit(solution)/shard_map/ppermute | solution.py:462
  15.3 2.3 %normed_rows.1 = (f32[1280,128]{1,0:T(8,128)S(1)}, s32[1,64]{1,0:T(1,128)S(1)}) custom-call(s32[4]{0:T(128)S(1)} %pad_add_fusion.1.place, bf16[80,2048]{1,0:T(8,128)(2,1)S(1)} %get-tuple-element.17.high, bf16[80,2048]{1,0:T(8,128)(2,1)S(1)} %get-tuple-element.18.low, f32[80,384]{1,0:T(8,128)S(1)} %collective-permute-done.got_a, ...), custom_call_target="tpu_custom_call" | custom-call | flops 629145600 | bytes 2621440 | tf_op jit(solution)/shard_map/normed_rows/pallas_call | solution.py:363
  17.6 0.0 collective-permute-done.5.refs_3_
  17.6 0.0 collective-permute-done.4
  17.6 2.3 %collective-permute-done.3 = bf16[240,128]{1,0:T(8,128)(2,1)S(1)} collective-permute-done((bf16[240,128]{1,0:T(8,128)(2,1)S(1)}, bf16[240,128]{1,0:T(8,128)(2,1)S(1)}, u32[]{:S(2)}, u32[]{:S(2)}) %collective-permute-start.3) | collective-permute-done | bytes 61472 | tf_op jit(solution)/shard_map/ppermute | solution.py:462
  20.0 0.0 collective-permute-done.2
  20.0 0.5 %collective-permute-start.6 = (bf16[720,128]{1,0:T(8,128)(2,1)S(1)}, bf16[720,128]{1,0:T(8,128)(2,1)S(1)}, u32[]{:S(2)}, u32[]{:S(2)}) collective-permute-start(bf16[720,128]{1,0:T(8,128)(2,1)S(1)} %constant_dynamic-update-slice_fusion.refs_2_), channel_id=1, source_target_pairs={{0,4},{4,0},{8,12},{12,8},{16,20},{20,16},{24,28},{28,24},{1,5},{5... | collective-permute-start | bytes 552968 | tf_op jit(solution)/shard_map/ppermute | solution.py:462
  20.5 3.5 %shifted_rows.1.refs_5_ = bf16[2560,2304]{1,0:T(8,128)(2,1)S(1)} custom-call(f32[1280,128]{1,0:T(8,128)S(1)} %get-tuple-element.28.normed), custom_call_target="tpu_custom_call" | custom-call | flops 23592960 | bytes 11796480 | tf_op jit(solution)/shard_map/shifted_rows/pallas_call | solution.py:384
  24.0 2.1 %collective-permute-done.6.refs_4_ = bf16[720,128]{1,0:T(8,128)(2,1)S(1)} collective-permute-done((bf16[720,128]{1,0:T(8,128)(2,1)S(1)}, bf16[720,128]{1,0:T(8,128)(2,1)S(1)}, u32[]{:S(2)}, u32[]{:S(2)}) %collective-permute-start.6) | collective-permute-done | bytes 184352 | tf_op jit(solution)/shard_map/ppermute | solution.py:462
  26.1 16.7 %correlate.1 = f32[64,10,4,8,128]{4,3,2,1,0:T(8,128)} custom-call(s32[1,64]{1,0:T(1,128)S(1)} %get-tuple-element.19.refs_0_, bf16[240,128]{1,0:T(8,128)(2,1)S(1)} %source_rows.1.refs_1_, bf16[720,128]{1,0:T(8,128)(2,1)S(1)} %constant_dynamic-update-slice_fusion.refs_2_, bf16[240,128]{1,0:T(8,128)(2,1)S(1)} %collective-permute-done.5.refs_3_, ...), custom_call_target="tpu_custom_call" | custom-call | tf_op jit(solution)/shard_map/correlate/pallas_call | solution.py:404
  (3 shorter events, 0.0 us)
Async XLA Ops:
  1.0 6.6 %collective-permute-start.1 = (f32[80,384]{1,0:T(8,128)S(1)}, f32[80,384]{1,0:T(8,128)S(1)}, u32[]{:S(2)}, u32[]{:S(2)}) collective-permute-start(f32[80,384]{1,0:T(8,128)S(1)} %get-tuple-element.29), channel_id=1, source_target_pairs={{0,3},{1,2},{2,1},{3,0},{4,7},{5,6},{6,5},{7,4},{8,11},{9,10},{10,... | collective-permute-start | bytes 368648 | tf_op jit(solution)/shard_map/ppermute | solution.py:450
  3.4 4.1 %collective-permute-start = (f32[80,384]{1,0:T(8,128)S(1)}, f32[80,384]{1,0:T(8,128)S(1)}, u32[]{:S(2)}, u32[]{:S(2)}) collective-permute-start(f32[80,384]{1,0:T(8,128)S(1)} %get-tuple-element.30), channel_id=1, source_target_pairs={{0,1},{1,0},{2,3},{3,2},{4,5},{5,4},{6,7},{7,6},{8,9},{9,8},{10,11... | collective-permute-start | bytes 368648 | tf_op jit(solution)/shard_map/ppermute | solution.py:451
  5.6 1.1 %copy-start = (f32[80,2048]{1,0:T(8,128)S(1)}, f32[80,2048]{1,0:T(8,128)}, u32[]{:S(2)}) copy-start(f32[80,2048]{1,0:T(8,128)} %traces.1) | copy-start | bytes 1966084
  8.9 8.8 %collective-permute-start.5 = (bf16[240,128]{1,0:T(8,128)(2,1)S(1)}, bf16[240,128]{1,0:T(8,128)(2,1)S(1)}, u32[]{:S(2)}, u32[]{:S(2)}) collective-permute-start(bf16[240,128]{1,0:T(8,128)(2,1)S(1)} %source_rows.1.refs_1_), channel_id=1, source_target_pairs={{0,4},{4,0},{8,12},{12,8},{16,20},{20,16},{24,28},{28,24},{1,5},{5... | collective-permute-start | bytes 184328 | tf_op jit(solution)/shard_map/ppermute | solution.py:462
  11.0 6.7 %collective-permute-start.4 = (bf16[240,128]{1,0:T(8,128)(2,1)S(1)}, bf16[240,128]{1,0:T(8,128)(2,1)S(1)}, u32[]{:S(2)}, u32[]{:S(2)}) collective-permute-start(bf16[240,128]{1,0:T(8,128)(2,1)S(1)} %source_rows.1.refs_1_), channel_id=1, source_target_pairs={{0,24},{4,28},{8,16},{12,20},{16,8},{20,12},{24,0},{28,4},{1,25},{... | collective-permute-start | bytes 184328 | tf_op jit(solution)/shard_map/ppermute | solution.py:462
  14.6 5.4 %collective-permute-start.3 = (bf16[240,128]{1,0:T(8,128)(2,1)S(1)}, bf16[240,128]{1,0:T(8,128)(2,1)S(1)}, u32[]{:S(2)}, u32[]{:S(2)}) collective-permute-start(bf16[240,128]{1,0:T(8,128)(2,1)S(1)} %source_rows.1.refs_1_), channel_id=1, source_target_pairs={{0,16},{4,20},{8,24},{12,28},{16,0},{20,4},{24,8},{28,12},{1,17},{... | collective-permute-start | bytes 184328 | tf_op jit(solution)/shard_map/ppermute | solution.py:462
  14.6 5.4 %collective-permute-start.2 = (bf16[240,128]{1,0:T(8,128)(2,1)S(1)}, bf16[240,128]{1,0:T(8,128)(2,1)S(1)}, u32[]{:S(2)}, u32[]{:S(2)}) collective-permute-start(bf16[240,128]{1,0:T(8,128)(2,1)S(1)} %source_rows.1.refs_1_), channel_id=1, source_target_pairs={{0,8},{4,12},{8,0},{12,4},{16,24},{20,28},{24,16},{28,20},{1,9},{5... | collective-permute-start | bytes 184328 | tf_op jit(solution)/shard_map/ppermute | solution.py:462
  20.0 6.1 %collective-permute-start.6 = (bf16[720,128]{1,0:T(8,128)(2,1)S(1)}, bf16[720,128]{1,0:T(8,128)(2,1)S(1)}, u32[]{:S(2)}, u32[]{:S(2)}) collective-permute-start(bf16[720,128]{1,0:T(8,128)(2,1)S(1)} %constant_dynamic-update-slice_fusion.refs_2_), channel_id=1, source_target_pairs={{0,4},{4,0},{8,12},{12,8},{16,20},{20,16},{24,28},{28,24},{1,5},{5... | collective-permute-start | bytes 552968 | tf_op jit(solution)/shard_map/ppermute | solution.py:462
